TPU v7x, 256 devices: a whole 4x4x8 slice. The times are simulated.
256 devices in a mesh: bricks: 64 (over y, z, core), pts: 4 (over x).
Axes of the slice: x: 4, y: 4, z: 8, core: 2. Of those that a mesh axis runs over, the one named last changes fastest.
Arguments:
- right_side: float32 [1024, 64, 128], P(('bricks', 'pts'))
- initial_guess: float32 [1024, 64, 128], P(('bricks', 'pts')), may hold values from -3 to 3
- point_cell: int32 [3, 524288], P(None, ('bricks', 'pts')), may hold values from 1 to 126, as said below
- point_offset: float32 [3, 524288], P(None, ('bricks', 'pts')), may hold values from -0.5 to 0.5
- point_weight: float32 [524288], P(('bricks', 'pts')), may hold values from 1 to 8
- point_mask: int32 [524288], P(('bricks', 'pts')), may hold values from 0 to 1, as said below
- block_count: int32 [256], P(('bricks', 'pts')), may hold values from 1 to 8, as said below
Outputs:
- solution_field: float32 [1024, 64, 128], P(('bricks', 'pts'))
- residual: float32 [1024, 64, 128], P(('bricks', 'pts'))
Inputs may be any that keep to these rules, and one draw needn't show every extreme that they name: `point_cell`: component 0 lies in 1 to 2, component 1 in 1 to 62, component 2 in 1 to 126, so that every point's 27 cells lie in its own device's slab. `point_mask`: within each aligned block of 256 points the ones come first. `block_count`: some device has all 8 blocks live in every draw.
All inputs are finite; a program needn't handle non-finite values.
Results may differ from a plain program's by a relative error of at most 0.0035.
Values sent between devices are 32-bit elements; how exact they have to be, the bound alone decides.
A program may use at most 64 MiB of HBM per device.

v0:
```python
import jax
import jax.numpy as jnp
from jax import lax
from jax.sharding import PartitionSpec as P

BLOCK = 256
ITERS = 2


MASS_TAPS = (1.0 / 120.0, 26.0 / 120.0, 66.0 / 120.0, 26.0 / 120.0, 1.0 / 120.0)
STIFF_TAPS = (-1.0 / 6.0, -1.0 / 3.0, 1.0, -1.0 / 3.0, -1.0 / 6.0)


def extended_2(cells, sides, width):
    for axis, dim in sides:
        count = lax.axis_size(axis)
        ends = count - 1
        head = lax.slice_in_dim(cells, 0, width, axis=dim)
        tail = lax.slice_in_dim(cells, cells.shape[dim] - width, cells.shape[dim], axis=dim)
        cells = jnp.concatenate(
            [
                lax.ppermute(tail, axis, [(i, (i + 1) % count) for i in range(ends)]),
                cells,
                lax.ppermute(head, axis, [((i + 1) % count, i) for i in range(ends)]),
            ],
            axis=dim,
        )
    return cells


def filter_axis(padded, tap_list, along):
    length = padded.shape[along] - 4
    summed = tap_list[0] * lax.slice_in_dim(padded, 0, length, axis=along)
    for offset in range(1, 5):
        summed = summed + tap_list[offset] * lax.slice_in_dim(
            padded, offset, offset + length, axis=along
        )
    return summed


def stencil(extended):
    padded = jnp.pad(extended, ((0, 0), (2, 2), (2, 2)))
    mass_z = filter_axis(padded, MASS_TAPS, 2)
    stiff_z = filter_axis(padded, STIFF_TAPS, 2)
    mass_yz = filter_axis(mass_z, MASS_TAPS, 1)
    cross_yz = filter_axis(mass_z, STIFF_TAPS, 1) + filter_axis(stiff_z, MASS_TAPS, 1)
    return filter_axis(mass_yz, STIFF_TAPS, 0) + filter_axis(cross_yz, MASS_TAPS, 0)


def spline_weights(offset):
    return (0.5 * (0.5 - offset) ** 2, 0.75 - offset * offset, 0.5 * (0.5 + offset) ** 2)


def axis_table(cell, offset, span):
    factors = spline_weights(offset)
    places = lax.broadcasted_iota(jnp.int32, (span, cell.shape[0]), 0)
    table = jnp.zeros((span, cell.shape[0]), jnp.float32)
    for step in range(3):
        table = table + jnp.where(places == (cell + step - 1)[None, :], factors[step][None, :], 0.0)
    return table


def screen_field(vector, point_cell, point_offset, strength):
    span_x, span_y, span_z = vector.shape
    total = strength.shape[0]
    width = min(512, total)
    number = total // width
    grid = vector.reshape(span_x * span_y, span_z)
    items = (
        point_cell[0].reshape(number, width),
        point_cell[1].reshape(number, width),
        point_cell[2].reshape(number, width),
        point_offset[0].reshape(number, width),
        point_offset[1].reshape(number, width),
        point_offset[2].reshape(number, width),
        strength.reshape(number, width),
    )

    def block_step(accumulated, item):
        first_cell, second_cell, third_cell, first_off, second_off, third_off, block_strength = item
        table_z = axis_table(third_cell, third_off, span_z)
        table_x = axis_table(first_cell, first_off, span_x)
        table_y = axis_table(second_cell, second_off, span_y)
        table_xy = (table_x[:, None, :] * table_y[None, :, :]).reshape(span_x * span_y, width)
        sampled = jnp.dot(
            grid, table_z, precision=lax.Precision.HIGHEST, preferred_element_type=jnp.float32
        )
        values = jnp.sum(sampled * table_xy, axis=0) * block_strength
        spread = table_xy * values[None, :]
        accumulated = accumulated + lax.dot_general(
            spread,
            table_z,
            (((1,), (1,)), ((), ())),
            precision=lax.Precision.HIGHEST,
            preferred_element_type=jnp.float32,
        )
        return (accumulated, None)

    result, unused = lax.scan(block_step, jnp.zeros_like(grid), items)
    return result.reshape(vector.shape)


def squares(residual):
    return lax.psum(jnp.sum(residual * residual), ("bricks", "pts"))


def body(
    right_side, initial_guess, point_cell, point_offset, point_weight, point_mask, block_count
):
    point_total = point_mask.shape[0]
    block_of = jnp.arange(point_total, dtype=jnp.int32) // BLOCK
    alive_mask = (block_of < block_count[0]) & (point_mask == 1)
    strength = jnp.where(alive_mask, point_weight, jnp.zeros_like(point_weight))

    def operate(vector):
        extended = extended_2(vector, ((("bricks", "pts"), 0),), 2)
        return stencil(extended) + screen_field(vector, point_cell, point_offset, strength)

    solution_field = initial_guess
    residual = right_side - operate(initial_guess)
    direction = residual
    norm_now = squares(residual)
    for step_index in range(ITERS):
        image = operate(direction)
        alpha = norm_now / lax.psum(jnp.sum(direction * image), ("bricks", "pts"))
        solution_field = solution_field + alpha * direction
        residual = residual - alpha * image
        norm_next = squares(residual)
        direction = residual + norm_next / norm_now * direction
        norm_now = norm_next
    return (solution_field, residual)


def solution(mesh):
    placed = (
        P(("bricks", "pts"), None, None),
        P(("bricks", "pts"), None, None),
        P(None, ("bricks", "pts")),
        P(None, ("bricks", "pts")),
        P(("bricks", "pts")),
        P(("bricks", "pts")),
        P(("bricks", "pts")),
    )
    return jax.shard_map(
        body,
        mesh=mesh,
        in_specs=placed,
        out_specs=(P(("bricks", "pts"), None, None), P(("bricks", "pts"), None, None)),
        check_vma=False,
    )
```

profile of v0, /device:TPU:1, one launch (start us, length us, event | category | flops | bytes accessed | tf_op | source)
XLA Modules:
  0.0 286.1 jit_solution(10363155383355835350)
XLA Ops:
  0.7 0.9 fusion.110
  1.6 4.1 %collective-permute-start = (f32[2,64,128]{2,1,0:T(8,128)S(1)}, f32[2,64,128]{2,1,0:T(8,128)S(1)}, u32[]{:S(2)}, u32[]{:S(2)}) collective-permute-start(f32[2,64,128]{2,1,0:T(8,128)S(1)} %get-tuple-element.981), channel_id=1, source_target_pairs={{0,1},{1,2},{2,3},{3,4},{4,5},{5,6},{6,7},{7,8},{8,9},{9,10},{10,1... | collective-permute-start | bytes 196616 | tf_op jit(solution)/shard_map/ppermute | solution.py:22
  5.7 3.7 %collective-permute-start.1 = (f32[2,64,128]{2,1,0:T(8,128)S(1)}, f32[2,64,128]{2,1,0:T(8,128)S(1)}, u32[]{:S(2)}, u32[]{:S(2)}) collective-permute-start(f32[2,64,128]{2,1,0:T(8,128)S(1)} %get-tuple-element.982), channel_id=1, source_target_pairs={{1,0},{2,1},{3,2},{4,3},{5,4},{6,5},{7,6},{8,7},{9,8},{10,9},{11,1... | collective-permute-start | bytes 196616 | tf_op jit(solution)/shard_map/ppermute | solution.py:24
  10.4 7.0 %while.48 = (s32[]{:T(128)}, f32[256,128]{1,0:T(8,128)S(1)}, s32[4,512]{1,0:T(4,128)S(1)}, f32[4,512]{1,0:T(4,128)S(1)}, s32[4,512]{1,0:T(4,128)S(1)}, /*index=5...) while((s32[]{:T(128)}, f32[256,128]{1,0:T(8,128)S(1)}, ...), condition=%wide.region_2.3_spmd.clone, body=%wide.region_0.2_spmd.clone.sunk | while | flops 404585472 | bytes 3408027 | solution.py:99
  10.7 0.7 fusion.128
  11.4 0.1 bitcast_multiply_fusion.6
  11.5 0.7 convolution_add_fusion.6
  12.4 0.7 fusion.128
  13.1 0.1 bitcast_multiply_fusion.6
  13.2 0.7 convolution_add_fusion.6
  14.2 0.7 fusion.128
  14.9 0.1 bitcast_multiply_fusion.6
  15.0 0.7 convolution_add_fusion.6
  15.9 0.7 fusion.128
  16.6 0.1 bitcast_multiply_fusion.6
  16.7 0.7 convolution_add_fusion.6
  17.4 0.2 select_maximum_fusion.4
  17.7 0.4 multiply_add_fusion.5
  18.0 0.4 multiply_add_fusion.8
  18.4 0.5 copy-done.1
  18.9 0.1 fusion.93
  19.1 1.9 collective-permute-start.2
  21.0 4.9 %collective-permute-start.3 = (f32[2,64,128]{2,1,0:T(8,128)S(1)}, f32[2,64,128]{2,1,0:T(8,128)S(1)}, u32[]{:S(2)}, u32[]{:S(2)}) collective-permute-start(f32[2,64,128]{2,1,0:T(8,128)S(1)} %get-tuple-element.980), channel_id=1, source_target_pairs={{1,0},{2,1},{3,2},{4,3},{5,4},{6,5},{7,6},{8,7},{9,8},{10,9},{11,1... | collective-permute-start | bytes 196616 | tf_op jit(solution)/shard_map/ppermute | solution.py:24
  25.9 7.0 %while.49 = (s32[]{:T(128)}, f32[256,128]{1,0:T(8,128)S(1)}, s32[4,512]{1,0:T(4,128)S(1)}, f32[4,512]{1,0:T(4,128)S(1)}, s32[4,512]{1,0:T(4,128)S(1)}, /*index=5...) while((s32[]{:T(128)}, f32[256,128]{1,0:T(8,128)S(1)}, ...), condition=%wide.region_7.8_spmd.clone, body=%wide.region_5.7_spmd.clone.sunk | while | flops 404585472 | bytes 3408027 | solution.py:99
  26.1 0.7 fusion.131
  26.9 0.1 bitcast_multiply_fusion.7
  26.9 0.7 convolution_add_fusion.7
  27.9 0.7 fusion.131
  28.6 0.1 bitcast_multiply_fusion.7
  28.7 0.7 convolution_add_fusion.7
  29.6 0.7 fusion.131
  30.4 0.1 bitcast_multiply_fusion.7
  30.4 0.7 convolution_add_fusion.7
  31.4 0.7 fusion.131
  32.1 0.1 bitcast_multiply_fusion.7
  32.2 0.7 convolution_add_fusion.7
  32.9 0.2 select_maximum_fusion.2
  33.1 0.4 multiply_add_fusion.3
  33.5 0.4 multiply_add_fusion.7
  33.9 0.8 multiply_reduce_fusion.2
  34.7 81.5 %all-reduce.3 = (f32[]{:T(128)}, f32[]{:T(128)}) all-reduce(f32[]{:T(128)} %get-tuple-element.831, f32[]{:T(128)} %get-tuple-element.830), channel_id=1, replica_groups=mesh['bricks'=64,'pts'=4] {'bricks','pts'}, use_global_device_ids=true, to_apply=%region_4.5 | all-reduce | flops 2 | bytes 16 | tf_op jit(solution)/shard_map/psum | solution.py:104
  117.4 0.6 multiply_reduce_fusion.1
  118.1 73.6 %psum.30 = f32[]{:T(128)} all-reduce(f32[]{:T(128)} %multiply_reduce_fusion.1), channel_id=1, replica_groups=mesh['bricks'=64,'pts'=4] {'bricks','pts'}, use_global_device_ids=true, to_apply=%region_11.12 | all-reduce | flops 1 | bytes 8 | tf_op jit(solution)/shard_map/psum | solution.py:104
  193.0 2.3 collective-permute-start.4
  195.3 4.5 %collective-permute-start.5 = (f32[2,64,128]{2,1,0:T(8,128)S(1)}, f32[2,64,128]{2,1,0:T(8,128)S(1)}, u32[]{:S(2)}, u32[]{:S(2)}) collective-permute-start(f32[2,64,128]{2,1,0:T(8,128)S(1)} %get-tuple-element.978), channel_id=1, source_target_pairs={{1,0},{2,1},{3,2},{4,3},{5,4},{6,5},{7,6},{8,7},{9,8},{10,9},{11,1... | collective-permute-start | bytes 196616 | tf_op jit(solution)/shard_map/ppermute | solution.py:24
  199.7 7.0 %while.50 = (s32[]{:T(128)}, f32[256,128]{1,0:T(8,128)S(1)}, s32[4,512]{1,0:T(4,128)S(1)}, f32[4,512]{1,0:T(4,128)S(1)}, s32[4,512]{1,0:T(4,128)S(1)}, /*index=5...) while((s32[]{:T(128)}, f32[256,128]{1,0:T(8,128)S(1)}, ...), condition=%wide.region_14.15_spmd.clone, body=%wide.region_12.14_spmd.clone.sunk | while | flops 404585472 | bytes 3408027 | solution.py:99
  200.0 0.7 fusion.134
  200.7 0.1 bitcast_multiply_fusion.8
  200.8 0.7 convolution_add_fusion.8
  201.8 0.7 fusion.134
  202.5 0.1 bitcast_multiply_fusion.8
  202.6 0.7 convolution_add_fusion.8
  203.5 0.7 fusion.134
  204.2 0.1 bitcast_multiply_fusion.8
  204.3 0.7 convolution_add_fusion.8
  205.3 0.7 fusion.134
  206.0 0.1 bitcast_multiply_fusion.8
  206.1 0.7 convolution_add_fusion.8
  206.8 0.2 select_maximum_fusion
  207.0 0.4 multiply_add_fusion.1
  207.4 0.4 multiply_add_fusion.6
  207.8 0.7 multiply_reduce_fusion
  208.5 75.5 %psum.31 = f32[]{:T(128)} all-reduce(f32[]{:T(128)} %get-tuple-element.918), channel_id=1, replica_groups=mesh['bricks'=64,'pts'=4] {'bricks','pts'}, use_global_device_ids=true, to_apply=%region_16.17 | all-reduce | flops 1 | bytes 8 | tf_op jit(solution)/shard_map/psum | solution.py:125
  285.4 0.7 multiply_subtract_fusion.9
  (165 shorter events, 2.6 us)
Async XLA Ops:
  0.6 9.5 %copy-start.4 = (f32[2048]{0:T(1024)S(1)}, f32[2048]{0:T(1024)}, u32[]{:S(2)}) copy-start(f32[2048]{0:T(1024)} %param.17) | copy-start | bytes 24580
  0.6 9.5 %copy-start.5 = (s32[2048]{0:T(1024)S(1)}, s32[2048]{0:T(1024)}, u32[]{:S(2)}) copy-start(s32[2048]{0:T(1024)} %param.18) | copy-start | bytes 24580
  0.7 9.6 %copy-start.3 = (f32[3,2048]{1,0:T(4,128)S(1)}, f32[3,2048]{1,0:T(4,128)}, u32[]{:S(2)}) copy-start(f32[3,2048]{1,0:T(4,128)} %param.16) | copy-start | bytes 73732
  1.6 8.6 %copy-start.2 = (s32[3,2048]{1,0:T(4,128)S(1)}, s32[3,2048]{1,0:T(4,128)}, u32[]{:S(2)}) copy-start(s32[3,2048]{1,0:T(4,128)} %param.15) | copy-start | bytes 73732
  1.6 8.8 %copy-start = (f32[4,64,128]{2,1,0:T(8,128)S(1)}, f32[4,64,128]{2,1,0:T(8,128)}, u32[]{:S(2)}) copy-start(f32[4,64,128]{2,1,0:T(8,128)} %param.14) | copy-start | bytes 393220
  1.6 15.8 %collective-permute-start = (f32[2,64,128]{2,1,0:T(8,128)S(1)}, f32[2,64,128]{2,1,0:T(8,128)S(1)}, u32[]{:S(2)}, u32[]{:S(2)}) collective-permute-start(f32[2,64,128]{2,1,0:T(8,128)S(1)} %get-tuple-element.981), channel_id=1, source_target_pairs={{0,1},{1,2},{2,3},{3,4},{4,5},{5,6},{6,7},{7,8},{8,9},{9,10},{10,1... | collective-permute-start | bytes 196616 | tf_op jit(solution)/shard_map/ppermute | solution.py:22
  5.7 11.7 %collective-permute-start.1 = (f32[2,64,128]{2,1,0:T(8,128)S(1)}, f32[2,64,128]{2,1,0:T(8,128)S(1)}, u32[]{:S(2)}, u32[]{:S(2)}) collective-permute-start(f32[2,64,128]{2,1,0:T(8,128)S(1)} %get-tuple-element.982), channel_id=1, source_target_pairs={{1,0},{2,1},{3,2},{4,3},{5,4},{6,5},{7,6},{8,7},{9,8},{10,9},{11,1... | collective-permute-start | bytes 196616 | tf_op jit(solution)/shard_map/ppermute | solution.py:24
  18.0 0.9 copy-start.1
  19.1 13.8 %collective-permute-start.2 = (f32[2,64,128]{2,1,0:T(8,128)S(1)}, f32[2,64,128]{2,1,0:T(8,128)S(1)}, u32[]{:S(2)}, u32[]{:S(2)}) collective-permute-start(f32[2,64,128]{2,1,0:T(8,128)S(1)} %get-tuple-element.979), channel_id=1, source_target_pairs={{0,1},{1,2},{2,3},{3,4},{4,5},{5,6},{6,7},{7,8},{8,9},{9,10},{10,1... | collective-permute-start | bytes 196616 | tf_op jit(solution)/shard_map/ppermute | solution.py:22
  21.0 11.9 %collective-permute-start.3 = (f32[2,64,128]{2,1,0:T(8,128)S(1)}, f32[2,64,128]{2,1,0:T(8,128)S(1)}, u32[]{:S(2)}, u32[]{:S(2)}) collective-permute-start(f32[2,64,128]{2,1,0:T(8,128)S(1)} %get-tuple-element.980), channel_id=1, source_target_pairs={{1,0},{2,1},{3,2},{4,3},{5,4},{6,5},{7,6},{8,7},{9,8},{10,9},{11,1... | collective-permute-start | bytes 196616 | tf_op jit(solution)/shard_map/ppermute | solution.py:24
  193.0 13.8 %collective-permute-start.4 = (f32[2,64,128]{2,1,0:T(8,128)S(1)}, f32[2,64,128]{2,1,0:T(8,128)S(1)}, u32[]{:S(2)}, u32[]{:S(2)}) collective-permute-start(f32[2,64,128]{2,1,0:T(8,128)S(1)} %get-tuple-element.977), channel_id=1, source_target_pairs={{0,1},{1,2},{2,3},{3,4},{4,5},{5,6},{6,7},{7,8},{8,9},{9,10},{10,1... | collective-permute-start | bytes 196616 | tf_op jit(solution)/shard_map/ppermute | solution.py:22
  195.3 11.5 %collective-permute-start.5 = (f32[2,64,128]{2,1,0:T(8,128)S(1)}, f32[2,64,128]{2,1,0:T(8,128)S(1)}, u32[]{:S(2)}, u32[]{:S(2)}) collective-permute-start(f32[2,64,128]{2,1,0:T(8,128)S(1)} %get-tuple-element.978), channel_id=1, source_target_pairs={{1,0},{2,1},{3,2},{4,3},{5,4},{6,5},{7,6},{8,7},{9,8},{10,9},{11,1... | collective-permute-start | bytes 196616 | tf_op jit(solution)/shard_map/ppermute | solution.py:24
where the time goes:
time: 287 us; the launch traced here: 286 us
  blocking collectives  231 us (80%)
  starting transfers between devices  21.4 us (7%)
  matrix products  16.5 us (6%)
  other arithmetic  9.06 us (3%)
  between operations  5.49 us (2%)
    psum x2, blocking collectives, squares(): return lax.psum(jnp.sum(residual * residual), ('bricks', 'pts'))  155 us
    psum x1, blocking collectives, body(): alpha = norm_now / lax.psum(jnp.sum(direction * image), ('bricks', 'pts'))  75.5 us
    ppermute x3, starting transfers between devices, extended_2(): lax.ppermute(head, axis, [((i + 1) % count, i) for i in range(ends)])  13.1 us
    dot_general x12, matrix products, block_step(): jnp.dot(grid, table_z, precision=lax.Precision.HIGHEST, preferred_element...  8.46 us
    ppermute x3, starting transfers between devices, extended_2(): lax.ppermute(tail, axis, [(i, (i + 1) % count) for i in range(ends)])  8.3 us
    dot_general x12, matrix products, block_step(): lax.dot_general(spread, table_z, (((1,), (1,)), ((), ())), precision=lax....  8 us
  transfers between devices with their start and end apart: 6, of which 0 were waited for; matrix products, arithmetic and copies ran while one was open for 7% of the time, Pallas kernels for 0%

commit v1 on v0

v1 whole, which is shorter than its diff:
```python
import functools

import jax
import jax.numpy as jnp
from jax import lax
from jax.experimental import pallas as pl
from jax.experimental.pallas import tpu as pltpu
from jax.sharding import PartitionSpec as P

MESH = pl.DeviceIdType.MESH

PLANES = 4
ROWS = 64
COLS = 128
CELLS = PLANES * ROWS
BLOCK = 256
BLOCKS = 8
POINTS = BLOCK * BLOCKS
EDGE = 8

SIZES = {"x": 4, "y": 4, "z": 8, "core": 2}
STAGES = (("x", "y"), ("z", "core"))


def spline_weights(offset):
    return (0.5 * (0.5 - offset) ** 2, 0.75 - offset * offset, 0.5 * (0.5 + offset) ** 2)


def coordinates():
    brick = lax.axis_index("bricks")
    return {
        "x": lax.axis_index("pts"),
        "y": brick // 16,
        "z": (brick // 2) % 8,
        "core": brick % 2,
    }


def device_of(place):
    return ((place["y"] * 8 + place["z"]) * 2 + place["core"], place["x"])


def stage_peers(here, axes):
    steps = [{}]
    for axis in axes:
        steps = [dict(step, **{axis: k}) for step in steps for k in range(SIZES[axis])]
    peers = []
    for step in steps[1:]:
        place = dict(here)
        for axis, k in step.items():
            if k:
                place[axis] = (here[axis] + k) % SIZES[axis]
        peers.append(device_of(place))
    return peers


def two_terms(value):
    high = value.astype(jnp.bfloat16)
    low = (value - high.astype(jnp.float32)).astype(jnp.bfloat16)
    return high, low


def block_row(ref, block):
    return jnp.concatenate([ref[2 * block : 2 * block + 1, :], ref[2 * block + 1 : 2 * block + 2, :]], axis=1)


def build_tables(cell_ref, offset_ref, weight_ref, mask_ref, count_ref, table_z, table_y, table_x, strength_ref):
    count = count_ref[0]
    for block in range(BLOCKS):
        lanes = pl.ds(block * BLOCK, BLOCK)

        def factors(axis):
            return cell_ref[axis : axis + 1, lanes], spline_weights(offset_ref[axis : axis + 1, lanes])

        def spread_out(cell, rows, parts):
            apart = lax.broadcasted_iota(jnp.int32, (rows, BLOCK), 0) - cell
            zero = jnp.zeros((rows, BLOCK), jnp.float32)
            before, at, after = apart == -1, apart == 0, apart == 1
            return [jnp.where(before, a, jnp.where(at, b, jnp.where(after, c, zero))) for a, b, c in parts]

        cell, parts = factors(2)
        terms = [two_terms(part) for part in parts]
        high, low = spread_out(
            cell,
            COLS,
            [[t[0].astype(jnp.float32) for t in terms], [t[1].astype(jnp.float32) for t in terms]],
        )
        table_z[0:COLS, lanes] = high.astype(jnp.bfloat16)
        table_z[COLS : 2 * COLS, lanes] = low.astype(jnp.bfloat16)
        cell, parts = factors(1)
        table_y[:, lanes] = spread_out(cell, ROWS, [parts])[0]
        cell, parts = factors(0)
        table_x[:, lanes] = spread_out(cell, 8, [parts])[0]
        alive = jnp.where(count > block, 1.0, 0.0)
        strength_ref[0:1, lanes] = (
            jnp.where(block_row(mask_ref, block) == 1, block_row(weight_ref, block), 0.0) * alive
        )


def screen(field, table_z, table_y, table_x, strength_ref, left_ref, spread_ref):
    high, low = two_terms(field)
    left_ref[0:CELLS, 0:COLS] = high
    left_ref[0:CELLS, COLS : 2 * COLS] = high
    left_ref[CELLS : 2 * CELLS, 0:COLS] = low
    left_ref[CELLS : 2 * CELLS, COLS : 2 * COLS] = low
    for block in range(BLOCKS):
        lanes = pl.ds(block * BLOCK, BLOCK)
        both = jnp.dot(left_ref[...], table_z[:, lanes], preferred_element_type=jnp.float32)
        sampled = (both[0:CELLS] + both[CELLS : 2 * CELLS]).reshape(PLANES, ROWS, BLOCK)
        along_y = table_y[:, lanes]
        along_x = table_x[:, lanes]
        total = jnp.zeros((8, BLOCK), jnp.float32)
        for plane in range(PLANES):
            summed = jnp.sum((sampled[plane] * along_y).reshape(ROWS // 8, 8, BLOCK), axis=0)
            total = total + summed * along_x[plane : plane + 1]
        values = jnp.sum(total, axis=0, keepdims=True) * strength_ref[0:1, lanes]
        for plane in range(PLANES):
            high, low = two_terms(along_y * (along_x[plane : plane + 1] * values))
            spread_ref[plane * ROWS : (plane + 1) * ROWS, lanes] = high
            spread_ref[CELLS + plane * ROWS : CELLS + (plane + 1) * ROWS, lanes] = low
    result = lax.dot_general(
        spread_ref[...], table_z[...], (((1,), (1,)), ((), ())), preferred_element_type=jnp.float32
    )
    result = result[0:CELLS] + result[CELLS : 2 * CELLS]
    return result[:, 0:COLS] + result[:, COLS : 2 * COLS]


def mass(values):
    return (66.0 / 120.0) * values[2] + (26.0 / 120.0) * (values[1] + values[3]) + (1.0 / 120.0) * (values[0] + values[4])


def stiff(values):
    return values[2] - (1.0 / 3.0) * (values[1] + values[3]) - (1.0 / 6.0) * (values[0] + values[4])


def stencil(field_ref, first, last, stiff_ref, mass_ref):
    planes = [field_ref[k] for k in range(PLANES + 4)]
    planes[0:2] = [jnp.where(first, 0.0, p) for p in planes[0:2]]
    planes[6:8] = [jnp.where(last, 0.0, p) for p in planes[6:8]]
    for k in range(PLANES):
        stiff_ref[k, EDGE : EDGE + ROWS, :] = stiff(planes[k : k + 5])
        mass_ref[k, EDGE : EDGE + ROWS, :] = mass(planes[k : k + 5])
    lane = lax.broadcasted_iota(jnp.int32, (ROWS, COLS), 1)

    def along_z(value):
        return [
            jnp.where(lane >= 2, pltpu.roll(value, 2, 1), 0.0),
            jnp.where(lane >= 1, pltpu.roll(value, 1, 1), 0.0),
            value,
            jnp.where(lane < COLS - 1, pltpu.roll(value, COLS - 1, 1), 0.0),
            jnp.where(lane < COLS - 2, pltpu.roll(value, COLS - 2, 1), 0.0),
        ]

    out = []
    for k in range(PLANES):
        stiff_x = [stiff_ref[k, EDGE - 2 + s : EDGE - 2 + s + ROWS, :] for s in range(5)]
        mass_x = [mass_ref[k, EDGE - 2 + s : EDGE - 2 + s + ROWS, :] for s in range(5)]
        out.append(mass(along_z(mass(stiff_x) + stiff(mass_x))) + stiff(along_z(mass(mass_x))))
    return out


def combine(tiles):
    largest = functools.reduce(jnp.maximum, [t[4:5] for t in tiles])
    total = jnp.zeros((8, COLS), jnp.float32)
    for t in tiles:
        ratio = t[4:5] / largest
        total = total + t * (ratio * ratio)
    row = lax.broadcasted_iota(jnp.int32, (8, COLS), 0)
    return jnp.where(row == 4, largest, total)


def kernel(
    right_ref, guess_ref, cell_ref, offset_ref, weight_ref, mask_ref, count_ref,
    out_field, out_residual,
    guess, residual, image, second, stiff_ref, mass_ref,
    table_z, table_y, table_x, strength_ref, left_ref, spread_ref,
    sums, arrived_a, arrived_b,
    halo_send, halo_recv, sum_send, sum_recv,
):
    here = coordinates()
    device = lax.axis_index("bricks") * 4 + lax.axis_index("pts")
    before, after = (device + 255) % 256, (device + 1) % 256
    left, right = (before // 4, before % 4), (after // 4, after % 4)
    peers = [stage_peers(here, axes) for axes in STAGES]

    barrier = pltpu.get_barrier_semaphore()
    greeted = [left, right] + [p for stage in peers for p in stage]
    for peer in greeted:
        pl.semaphore_signal(barrier, inc=1, device_id=peer, device_id_type=MESH)

    guess[2:6] = guess_ref[...]
    for ref in (stiff_ref, mass_ref):
        ref[:, 0:EDGE, :] = jnp.zeros((PLANES, EDGE, COLS), jnp.float32)
        ref[:, EDGE + ROWS : 2 * EDGE + ROWS, :] = jnp.zeros((PLANES, EDGE, COLS), jnp.float32)
    build_tables(cell_ref, offset_ref, weight_ref, mask_ref, count_ref, table_z, table_y, table_x, strength_ref)
    tables = (table_z, table_y, table_x, strength_ref, left_ref, spread_ref)

    pl.semaphore_wait(barrier, len(greeted))

    def exchange(field, turn):
        copies = []
        for side, (source, target, to) in enumerate(((2, 6, left), (4, 0, right))):
            copy = pltpu.make_async_remote_copy(
                src_ref=field.at[pl.ds(source, 2)],
                dst_ref=field.at[pl.ds(target, 2)],
                send_sem=halo_send.at[turn, side],
                recv_sem=halo_recv.at[turn, side],
                device_id=to,
                device_id_type=MESH,
            )
            copy.start()
            copies.append(copy)
        return copies

    def operate(field, turn):
        copies = exchange(field, turn)
        screened = screen(field[2:6].reshape(CELLS, COLS), *tables).reshape(PLANES, ROWS, COLS)
        second[...] = screened
        for copy in copies:
            copy.wait_recv()
        smooth = stencil(field, device == 0, device == 255, stiff_ref, mass_ref)
        return copies, [smooth[k] + second[k] for k in range(PLANES)]

    started = []
    copies, product = operate(guess, 0)
    started += copies
    for k in range(PLANES):
        residual[2 + k] = right_ref[k] - product[k]
    copies, product = operate(residual, 1)
    started += copies
    for k in range(PLANES):
        image[2 + k] = product[k]
    copies, product = operate(image, 2)
    started += copies
    for k in range(PLANES):
        second[k] = product[k]

    def fold(value):
        return value.reshape(CELLS // 8, 8, COLS)

    r0 = fold(residual[2:6])
    scale = jnp.max(jnp.max(jnp.abs(r0), axis=0), axis=0, keepdims=True)
    scale = jnp.maximum(scale, 1e-30)
    inverse = 1.0 / scale
    r0 = r0 * inverse
    w = fold(image[2:6]) * inverse
    u = fold(second[...]) * inverse
    row = lax.broadcasted_iota(jnp.int32, (8, COLS), 0)
    tile = jnp.where(row == 4, scale, 0.0)
    for k, (a, b) in enumerate(((r0, r0), (r0, w), (w, w), (w, u))):
        moment = jnp.sum(jnp.sum(a * b, axis=0), axis=0, keepdims=True)
        tile = jnp.where(row == k, moment, tile)

    for turn, arrived in enumerate((arrived_a, arrived_b)):
        sums[turn] = tile
        for slot, peer in enumerate(peers[turn]):
            copy = pltpu.make_async_remote_copy(
                src_ref=sums.at[turn],
                dst_ref=arrived.at[slot],
                send_sem=sum_send.at[turn],
                recv_sem=sum_recv.at[turn],
                device_id=peer,
                device_id_type=MESH,
            )
            copy.start()
        pltpu.make_async_copy(arrived, arrived, sum_recv.at[turn]).wait()
        tile = combine([tile] + [arrived[slot] for slot in range(len(peers[turn]))])

    top = tile[4:5]
    ratio = top / jnp.max(top, axis=1, keepdims=True)
    moments = jnp.sum(tile * (ratio * ratio), axis=1, keepdims=True)
    m0, m1, m2, m3 = (moments[k : k + 1] for k in range(4))
    a0 = m0 / m1
    g = a0 * (m2 / m1)
    a1 = (g - 1.0) * m1 / (a0 * m3 - g * m2)
    c1 = a0 + a1 * g
    c2 = a1 * a0
    for k in range(PLANES):
        out_field[k] = guess[2 + k] + c1 * residual[2 + k] - c2 * image[2 + k]
        out_residual[k] = residual[2 + k] - c1 * image[2 + k] + c2 * second[k]

    for copy in started:
        copy.wait_send()
    for turn, arrived in enumerate((arrived_a, arrived_b)):
        pltpu.make_async_copy(arrived, arrived, sum_send.at[turn]).wait()


def body(right_side, initial_guess, point_cell, point_offset, point_weight, point_mask, block_count):
    slab = jax.ShapeDtypeStruct((PLANES, ROWS, COLS), jnp.float32)
    vmem = pl.BlockSpec(memory_space=pltpu.VMEM)
    groups = []
    for axes in STAGES:
        size = 1
        for axis in axes:
            size *= SIZES[axis]
        groups.append(size - 1)
    return pl.pallas_call(
        kernel,
        out_shape=(slab, slab),
        in_specs=[vmem] * 6 + [pl.BlockSpec(memory_space=pltpu.SMEM)],
        out_specs=(vmem, vmem),
        scratch_shapes=[
            pltpu.VMEM((PLANES + 4, ROWS, COLS), jnp.float32),
            pltpu.VMEM((PLANES + 4, ROWS, COLS), jnp.float32),
            pltpu.VMEM((PLANES + 4, ROWS, COLS), jnp.float32),
            pltpu.VMEM((PLANES, ROWS, COLS), jnp.float32),
            pltpu.VMEM((PLANES, ROWS + 2 * EDGE, COLS), jnp.float32),
            pltpu.VMEM((PLANES, ROWS + 2 * EDGE, COLS), jnp.float32),
            pltpu.VMEM((2 * COLS, POINTS), jnp.bfloat16),
            pltpu.VMEM((ROWS, POINTS), jnp.float32),
            pltpu.VMEM((8, POINTS), jnp.float32),
            pltpu.VMEM((8, POINTS), jnp.float32),
            pltpu.VMEM((2 * CELLS, 2 * COLS), jnp.bfloat16),
            pltpu.VMEM((2 * CELLS, POINTS), jnp.bfloat16),
            pltpu.VMEM((2, 8, COLS), jnp.float32),
            pltpu.VMEM((groups[0], 8, COLS), jnp.float32),
            pltpu.VMEM((groups[1], 8, COLS), jnp.float32),
            pltpu.SemaphoreType.DMA((3, 2)),
            pltpu.SemaphoreType.DMA((3, 2)),
            pltpu.SemaphoreType.DMA((2,)),
            pltpu.SemaphoreType.DMA((2,)),
        ],
        compiler_params=pltpu.CompilerParams(
            collective_id=0, has_side_effects=True, vmem_limit_bytes=32 * 1024 * 1024
        ),
        cost_estimate=pl.CostEstimate(flops=3_000_000_000, bytes_accessed=700_000, transcendentals=0),
    )(
        right_side, initial_guess, point_cell, point_offset,
        point_weight.reshape(16, 128), point_mask.reshape(16, 128), block_count,
    )


def solution(mesh):
    placed = (
        P(("bricks", "pts"), None, None),
        P(("bricks", "pts"), None, None),
        P(None, ("bricks", "pts")),
        P(None, ("bricks", "pts")),
        P(("bricks", "pts")),
        P(("bricks", "pts")),
        P(("bricks", "pts")),
    )
    return jax.shard_map(
        body,
        mesh=mesh,
        in_specs=placed,
        out_specs=(P(("bricks", "pts"), None, None), P(("bricks", "pts"), None, None)),
        check_vma=False,
    )
```

time: 287 us -> 43 us (0.15)
  blocking collectives: 231 us -> 0 us
  Pallas kernels: 0 us -> 35.4 us
  starting transfers between devices: 21.4 us -> 0 us
  matrix products: 16.5 us -> 0 us
  other arithmetic: 9.06 us -> 0 us
  local copies, waits for them, and re-layouts: 1.66 us -> 6.02 us
  between operations: 5.49 us -> 1.3 us
    psum x3 -> x0, blocking collectives: 231 us -> none  [the longest x2 155 us: squares(): return lax.psum(jnp.sum(residual * residual), ('bricks', 'pts'))]
    pallas_call x0 -> x1, Pallas kernels: none -> 35.4 us  [body(): pl.pallas_call(kernel, out_shape=(slab, slab), in_specs=[vmem] * 6 + [pl....]
    ppermute x6 -> x0, starting transfers between devices: 21.4 us -> none  [the longest x3 13.1 us: extended_2(): lax.ppermute(head, axis, [((i + 1) % count, i) for i in range(ends)])]
    dot_general x24 -> x0, matrix products: 16.5 us -> none  [the longest x12 8.46 us: block_step(): jnp.dot(grid, table_z, precision=lax.Precision.HIGHEST, preferred_element...]
    unnamed x12 -> x14, local copies, waits for them, and re-layouts: 0.55 us -> 6.02 us
    add x31 -> x0, other arithmetic: 2.89 us -> none  [the longest x6 2.22 us: filter_axis(): summed + tap_list[offset] * lax.slice_in_dim(padded, offset, offset + len...]
  transfers between devices with their start and end apart: 6 -> 0, of which waited for: 0 -> 0; matrix products, arithmetic and copies ran while one was open for 7% -> 0% of each run, Pallas kernels for 0% -> 0%
where the time goes in v1:
time: 43 us; the launch traced here: 42.7 us
  Pallas kernels  35.4 us (82%)
  local copies, waits for them, and re-layouts  6.02 us (14%)
  between operations  1.3 us (3%)
    pallas_call x1, Pallas kernels, body(): pl.pallas_call(kernel, out_shape=(slab, slab), in_specs=[vmem] * 6 + [pl....  35.4 us
    unnamed x14, local copies, waits for them, and re-layouts  6.02 us

profile of v1, /device:TPU:1, one launch (start us, length us, event | category | flops | bytes accessed | tf_op | source)
XLA Modules:
  0.0 42.7 jit_solution(2164124919706819824)
XLA Ops:
  1.3 0.0 copy-start
  1.3 0.9 %copy-done = f32[4,64,128]{2,1,0:T(8,128)S(1)} copy-done((f32[4,64,128]{2,1,0:T(8,128)S(1)}, f32[4,64,128]{2,1,0:T(8,128)}, u32[]{:S(2)}) %copy-start) | copy-done | bytes 131096
  2.2 0.0 copy-start.1
  2.2 0.9 %copy-done.1 = f32[4,64,128]{2,1,0:T(8,128)S(1)} copy-done((f32[4,64,128]{2,1,0:T(8,128)S(1)}, f32[4,64,128]{2,1,0:T(8,128)}, u32[]{:S(2)}) %copy-start.1) | copy-done | bytes 131096
  3.1 0.0 copy-start.2
  3.1 0.8 %copy-done.2 = s32[3,2048]{1,0:T(4,128)S(1)} copy-done((s32[3,2048]{1,0:T(4,128)S(1)}, s32[3,2048]{1,0:T(4,128)}, u32[]{:S(2)}) %copy-start.2) | copy-done | bytes 24600
  3.8 0.0 copy-start.3
  3.8 0.8 %copy-done.3 = f32[3,2048]{1,0:T(4,128)S(1)} copy-done((f32[3,2048]{1,0:T(4,128)S(1)}, f32[3,2048]{1,0:T(4,128)}, u32[]{:S(2)}) %copy-start.3) | copy-done | bytes 24600
  4.6 0.0 copy-start.4
  4.6 0.7 %copy-done.4 = f32[2048]{0:T(1024)S(1)} copy-done((f32[2048]{0:T(1024)S(1)}, f32[2048]{0:T(1024)}, u32[]{:S(2)}) %copy-start.4) | copy-done | bytes 8216
  5.3 0.0 copy-start.5
  5.3 0.7 %copy-done.5 = s32[2048]{0:T(1024)S(1)} copy-done((s32[2048]{0:T(1024)S(1)}, s32[2048]{0:T(1024)}, u32[]{:S(2)}) %copy-start.5) | copy-done | bytes 8216
  6.0 35.4 %shard_map.86 = (f32[4,64,128]{2,1,0:T(8,128)S(1)}, f32[4,64,128]{2,1,0:T(8,128)S(1)}) custom-call(f32[4,64,128]{2,1,0:T(8,128)S(1)} %copy-done, f32[4,64,128]{2,1,0:T(8,128)S(1)} %copy-done.1, s32[3,2048]{1,0:T(4,128)S(1)} %copy-done.2, f32[3,2048]{1,0:T(4,128)S(1)} %copy-done.3, f32[16,128]{1,0:T(8,128)S(1)} %bitcast.2, s32[16,128]{1,0:T(8,128)S(1)} %bitcast.3, ...), custom_call_target="tpu_custom_call" | custom-call | flops 3000000000 | bytes 700000 | tf_op jit(solution)/shard_map/pallas_call | solution.py:297
  41.4 0.7 %copy.12 = f32[4,64,128]{2,1,0:T(8,128)} copy(f32[4,64,128]{2,1,0:T(8,128)S(1)} %get-tuple-element.4) | data formatting | bytes 262144
  42.0 0.7 %copy.13 = f32[4,64,128]{2,1,0:T(8,128)} copy(f32[4,64,128]{2,1,0:T(8,128)S(1)} %get-tuple-element.5) | data formatting | bytes 262144
Async XLA Ops:
  1.3 0.9 %copy-start = (f32[4,64,128]{2,1,0:T(8,128)S(1)}, f32[4,64,128]{2,1,0:T(8,128)}, u32[]{:S(2)}) copy-start(f32[4,64,128]{2,1,0:T(8,128)} %right_ref.1) | copy-start | bytes 393220
  2.2 0.9 %copy-start.1 = (f32[4,64,128]{2,1,0:T(8,128)S(1)}, f32[4,64,128]{2,1,0:T(8,128)}, u32[]{:S(2)}) copy-start(f32[4,64,128]{2,1,0:T(8,128)} %guess_ref.1) | copy-start | bytes 393220
  3.1 0.8 %copy-start.2 = (s32[3,2048]{1,0:T(4,128)S(1)}, s32[3,2048]{1,0:T(4,128)}, u32[]{:S(2)}) copy-start(s32[3,2048]{1,0:T(4,128)} %cell_ref.1) | copy-start | bytes 73732
  3.8 0.8 %copy-start.3 = (f32[3,2048]{1,0:T(4,128)S(1)}, f32[3,2048]{1,0:T(4,128)}, u32[]{:S(2)}) copy-start(f32[3,2048]{1,0:T(4,128)} %offset_ref.1) | copy-start | bytes 73732
  4.6 0.7 %copy-start.4 = (f32[2048]{0:T(1024)S(1)}, f32[2048]{0:T(1024)}, u32[]{:S(2)}) copy-start(f32[2048]{0:T(1024)} %param.11) | copy-start | bytes 24580
  5.3 0.7 %copy-start.5 = (s32[2048]{0:T(1024)S(1)}, s32[2048]{0:T(1024)}, u32[]{:S(2)}) copy-start(s32[2048]{0:T(1024)} %param.12) | copy-start | bytes 24580

commit v2 on v1

--- a/solution.py
+++ b/solution.py
@@ -19,7 +19,7 @@
 EDGE = 8
 
 SIZES = {"x": 4, "y": 4, "z": 8, "core": 2}
-STAGES = (("x", "y"), ("z", "core"))
+STAGES = (("x", "y", "core"), ("z",))
 
 
 def spline_weights(offset):
@@ -133,11 +133,9 @@
     return values[2] - (1.0 / 3.0) * (values[1] + values[3]) - (1.0 / 6.0) * (values[0] + values[4])
 
 
-def stencil(field_ref, first, last, stiff_ref, mass_ref):
-    planes = [field_ref[k] for k in range(PLANES + 4)]
-    planes[0:2] = [jnp.where(first, 0.0, p) for p in planes[0:2]]
-    planes[6:8] = [jnp.where(last, 0.0, p) for p in planes[6:8]]
-    for k in range(PLANES):
+def stencil(planes, stiff_ref, mass_ref):
+    count = len(planes) - 4
+    for k in range(count):
         stiff_ref[k, EDGE : EDGE + ROWS, :] = stiff(planes[k : k + 5])
         mass_ref[k, EDGE : EDGE + ROWS, :] = mass(planes[k : k + 5])
     lane = lax.broadcasted_iota(jnp.int32, (ROWS, COLS), 1)
@@ -152,31 +150,55 @@
         ]
 
     out = []
-    for k in range(PLANES):
+    for k in range(count):
         stiff_x = [stiff_ref[k, EDGE - 2 + s : EDGE - 2 + s + ROWS, :] for s in range(5)]
         mass_x = [mass_ref[k, EDGE - 2 + s : EDGE - 2 + s + ROWS, :] for s in range(5)]
         out.append(mass(along_z(mass(stiff_x) + stiff(mass_x))) + stiff(along_z(mass(mass_x))))
     return out
 
 
-def combine(tiles):
-    largest = functools.reduce(jnp.maximum, [t[4:5] for t in tiles])
-    total = jnp.zeros((8, COLS), jnp.float32)
-    for t in tiles:
-        ratio = t[4:5] / largest
-        total = total + t * (ratio * ratio)
-    row = lax.broadcasted_iota(jnp.int32, (8, COLS), 0)
-    return jnp.where(row == 4, largest, total)
+def packed(moments, scale):
+    lane = lax.broadcasted_iota(jnp.int32, (1, COLS), 1)
+    row = jnp.broadcast_to(scale, (1, COLS))
+    for k, moment in enumerate(moments):
+        for shift in (64, 32, 16):
+            moment = moment + pltpu.roll(moment, shift, 1)
+        row = jnp.where(lane // 16 == k, moment, row)
+    return row
+
+
+def combine(rows):
+    lane = lax.broadcasted_iota(jnp.int32, rows.shape, 1)
+    scales = jnp.max(jnp.where(lane >= 64, rows, 0.0), axis=1, keepdims=True)
+    largest = jnp.max(scales, axis=0, keepdims=True)
+    ratio = scales / largest
+    total = jnp.sum(rows * (ratio * ratio), axis=0, keepdims=True)
+    return jnp.where(lane[0:1] >= 64, largest, total)
 
 
 def kernel(
-    right_ref, guess_ref, cell_ref, offset_ref, weight_ref, mask_ref, count_ref,
+    right_in, guess_in, cell_in, offset_in, weight_in, mask_in, count_ref,
     out_field, out_residual,
-    guess, residual, image, second, stiff_ref, mass_ref,
+    right_ref, cell_ref, offset_ref, weight_ref, mask_ref,
+    guess, known, residual, image, second, stiff_ref, mass_ref,
     table_z, table_y, table_x, strength_ref, left_ref, spread_ref,
     sums, arrived_a, arrived_b,
-    halo_send, halo_recv, sum_send, sum_recv,
+    load_sem, halo_send, halo_recv, sum_send, sum_recv,
 ):
+    loads = [
+        pltpu.make_async_copy(source, target, load_sem.at[k])
+        for k, (source, target) in enumerate((
+            (cell_in, cell_ref),
+            (offset_in, offset_ref),
+            (weight_in, weight_ref),
+            (mask_in, mask_ref),
+            (guess_in, guess.at[pl.ds(4, PLANES)]),
+            (right_in, right_ref),
+        ))
+    ]
+    for load in loads:
+        load.start()
+
     here = coordinates()
     device = lax.axis_index("bricks") * 4 + lax.axis_index("pts")
     before, after = (device + 255) % 256, (device + 1) % 256
@@ -188,101 +210,132 @@
     for peer in greeted:
         pl.semaphore_signal(barrier, inc=1, device_id=peer, device_id_type=MESH)
 
-    guess[2:6] = guess_ref[...]
+    first, last = device == 0, device == 255
     for ref in (stiff_ref, mass_ref):
         ref[:, 0:EDGE, :] = jnp.zeros((PLANES, EDGE, COLS), jnp.float32)
         ref[:, EDGE + ROWS : 2 * EDGE + ROWS, :] = jnp.zeros((PLANES, EDGE, COLS), jnp.float32)
+    for load in loads[0:4]:
+        load.wait()
     build_tables(cell_ref, offset_ref, weight_ref, mask_ref, count_ref, table_z, table_y, table_x, strength_ref)
     tables = (table_z, table_y, table_x, strength_ref, left_ref, spread_ref)
 
+    loads[4].wait()
     pl.semaphore_wait(barrier, len(greeted))
-
-    def exchange(field, turn):
+    started = []
+
+    def send(field, turn, moves):
         copies = []
-        for side, (source, target, to) in enumerate(((2, 6, left), (4, 0, right))):
+        for side, (source, target) in enumerate(moves):
             copy = pltpu.make_async_remote_copy(
                 src_ref=field.at[pl.ds(source, 2)],
                 dst_ref=field.at[pl.ds(target, 2)],
                 send_sem=halo_send.at[turn, side],
                 recv_sem=halo_recv.at[turn, side],
-                device_id=to,
+                device_id=(left, right)[side],
                 device_id_type=MESH,
             )
             copy.start()
             copies.append(copy)
+        started.extend(copies)
         return copies
 
-    def operate(field, turn):
-        copies = exchange(field, turn)
-        screened = screen(field[2:6].reshape(CELLS, COLS), *tables).reshape(PLANES, ROWS, COLS)
-        second[...] = screened
+    def landed(copies):
         for copy in copies:
             copy.wait_recv()
-        smooth = stencil(field, device == 0, device == 255, stiff_ref, mass_ref)
-        return copies, [smooth[k] + second[k] for k in range(PLANES)]
-
-    started = []
-    copies, product = operate(guess, 0)
-    started += copies
+
+    def screened(field):
+        return screen(field.reshape(CELLS, COLS), *tables).reshape(PLANES, ROWS, COLS)
+
+    def outside(planes, side):
+        return [jnp.where(side, 0.0, p) for p in planes]
+
+    near = send(guess, 0, ((4, 8), (6, 2)))
+    far = send(guess, 1, ((6, 10), (4, 0)))
+    value = screened(guess[4:8])
+    loads[5].wait()
+    known[2:6] = right_ref[...] - value
+    edge = send(known, 2, ((2, 6), (4, 0)))
+
+    landed(near)
+    planes = outside([guess[k] for k in (2, 3)], first) + [guess[k] for k in range(4, 8)]
+    planes = planes + outside([guess[k] for k in (8, 9)], last)
+    smooth = stencil(planes, stiff_ref, mass_ref)
     for k in range(PLANES):
-        residual[2 + k] = right_ref[k] - product[k]
-    copies, product = operate(residual, 1)
-    started += copies
+        residual[2 + k] = known[2 + k] - smooth[k]
+    second[...] = screened(residual[2:6])
+
+    landed(far)
+    landed(edge)
+    smooth = stencil([guess[k] for k in range(0, 6)], stiff_ref, mass_ref)
+    for k in range(2):
+        residual[k] = jnp.where(first, 0.0, known[k] - smooth[k])
+    smooth = stencil([guess[k] for k in range(6, 12)], stiff_ref, mass_ref)
+    for k in range(2):
+        residual[6 + k] = jnp.where(last, 0.0, known[6 + k] - smooth[k])
+    smooth = stencil([residual[k] for k in range(8)], stiff_ref, mass_ref)
     for k in range(PLANES):
-        image[2 + k] = product[k]
-    copies, product = operate(image, 2)
-    started += copies
+        image[2 + k] = smooth[k] + second[k]
+    edge = send(image, 3, ((2, 6), (4, 0)))
+
+    value = screened(image[2:6])
+    second[...] = value
+    landed(edge)
+    planes = outside([image[k] for k in (0, 1)], first) + [image[k] for k in range(2, 6)]
+    planes = planes + outside([image[k] for k in (6, 7)], last)
+    smooth = stencil(planes, stiff_ref, mass_ref)
     for k in range(PLANES):
-        second[k] = product[k]
+        second[k] = second[k] + smooth[k]
 
     def fold(value):
         return value.reshape(CELLS // 8, 8, COLS)
 
     r0 = fold(residual[2:6])
     scale = jnp.max(jnp.max(jnp.abs(r0), axis=0), axis=0, keepdims=True)
-    scale = jnp.maximum(scale, 1e-30)
+    scale = jnp.maximum(jnp.max(scale, axis=1, keepdims=True), 1e-30)
     inverse = 1.0 / scale
     r0 = r0 * inverse
     w = fold(image[2:6]) * inverse
     u = fold(second[...]) * inverse
-    row = lax.broadcasted_iota(jnp.int32, (8, COLS), 0)
-    tile = jnp.where(row == 4, scale, 0.0)
-    for k, (a, b) in enumerate(((r0, r0), (r0, w), (w, w), (w, u))):
-        moment = jnp.sum(jnp.sum(a * b, axis=0), axis=0, keepdims=True)
-        tile = jnp.where(row == k, moment, tile)
+    moments = [
+        jnp.sum(jnp.sum(a * b, axis=0), axis=0, keepdims=True) for a, b in ((r0, r0), (r0, w), (w, w), (w, u))
+    ]
+    row = packed(moments, scale)
 
     for turn, arrived in enumerate((arrived_a, arrived_b)):
-        sums[turn] = tile
+        count = len(peers[turn])
+        sums[turn] = row
+        arrived[count : count + 1, :] = row
         for slot, peer in enumerate(peers[turn]):
-            copy = pltpu.make_async_remote_copy(
+            pltpu.make_async_remote_copy(
                 src_ref=sums.at[turn],
-                dst_ref=arrived.at[slot],
+                dst_ref=arrived.at[pl.ds(slot, 1)],
                 send_sem=sum_send.at[turn],
                 recv_sem=sum_recv.at[turn],
                 device_id=peer,
                 device_id_type=MESH,
-            )
-            copy.start()
-        pltpu.make_async_copy(arrived, arrived, sum_recv.at[turn]).wait()
-        tile = combine([tile] + [arrived[slot] for slot in range(len(peers[turn]))])
-
-    top = tile[4:5]
-    ratio = top / jnp.max(top, axis=1, keepdims=True)
-    moments = jnp.sum(tile * (ratio * ratio), axis=1, keepdims=True)
-    m0, m1, m2, m3 = (moments[k : k + 1] for k in range(4))
+            ).start()
+        whole = arrived.at[pl.ds(0, count)]
+        pltpu.make_async_copy(whole, whole, sum_recv.at[turn]).wait()
+        row = combine(arrived[...])
+
+    lane = lax.broadcasted_iota(jnp.int32, (1, COLS), 1)
+    m0, m1, m2, m3 = (
+        jnp.sum(jnp.where(lane // 16 == k, row, 0.0), axis=1, keepdims=True) for k in range(4)
+    )
     a0 = m0 / m1
     g = a0 * (m2 / m1)
     a1 = (g - 1.0) * m1 / (a0 * m3 - g * m2)
     c1 = a0 + a1 * g
     c2 = a1 * a0
     for k in range(PLANES):
-        out_field[k] = guess[2 + k] + c1 * residual[2 + k] - c2 * image[2 + k]
+        out_field[k] = guess[4 + k] + c1 * residual[2 + k] - c2 * image[2 + k]
         out_residual[k] = residual[2 + k] - c1 * image[2 + k] + c2 * second[k]
 
     for copy in started:
         copy.wait_send()
     for turn, arrived in enumerate((arrived_a, arrived_b)):
-        pltpu.make_async_copy(arrived, arrived, sum_send.at[turn]).wait()
+        whole = arrived.at[pl.ds(0, len(peers[turn]))]
+        pltpu.make_async_copy(whole, whole, sum_send.at[turn]).wait()
 
 
 def body(right_side, initial_guess, point_cell, point_offset, point_weight, point_mask, block_count):
@@ -293,13 +346,19 @@
         size = 1
         for axis in axes:
             size *= SIZES[axis]
-        groups.append(size - 1)
+        groups.append(size)
     return pl.pallas_call(
         kernel,
         out_shape=(slab, slab),
-        in_specs=[vmem] * 6 + [pl.BlockSpec(memory_space=pltpu.SMEM)],
+        in_specs=[pl.BlockSpec(memory_space=pltpu.HBM)] * 6 + [pl.BlockSpec(memory_space=pltpu.SMEM)],
         out_specs=(vmem, vmem),
         scratch_shapes=[
+            pltpu.VMEM((PLANES, ROWS, COLS), jnp.float32),
+            pltpu.VMEM((3, POINTS), jnp.int32),
+            pltpu.VMEM((3, POINTS), jnp.float32),
+            pltpu.VMEM((POINTS // COLS, COLS), jnp.float32),
+            pltpu.VMEM((POINTS // COLS, COLS), jnp.int32),
+            pltpu.VMEM((PLANES + 8, ROWS, COLS), jnp.float32),
             pltpu.VMEM((PLANES + 4, ROWS, COLS), jnp.float32),
             pltpu.VMEM((PLANES + 4, ROWS, COLS), jnp.float32),
             pltpu.VMEM((PLANES + 4, ROWS, COLS), jnp.float32),
@@ -312,21 +371,22 @@
             pltpu.VMEM((8, POINTS), jnp.float32),
             pltpu.VMEM((2 * CELLS, 2 * COLS), jnp.bfloat16),
             pltpu.VMEM((2 * CELLS, POINTS), jnp.bfloat16),
-            pltpu.VMEM((2, 8, COLS), jnp.float32),
-            pltpu.VMEM((groups[0], 8, COLS), jnp.float32),
-            pltpu.VMEM((groups[1], 8, COLS), jnp.float32),
-            pltpu.SemaphoreType.DMA((3, 2)),
-            pltpu.SemaphoreType.DMA((3, 2)),
+            pltpu.VMEM((2, 1, COLS), jnp.float32),
+            pltpu.VMEM((groups[0], COLS), jnp.float32),
+            pltpu.VMEM((groups[1], COLS), jnp.float32),
+            pltpu.SemaphoreType.DMA((6,)),
+            pltpu.SemaphoreType.DMA((4, 2)),
+            pltpu.SemaphoreType.DMA((4, 2)),
             pltpu.SemaphoreType.DMA((2,)),
             pltpu.SemaphoreType.DMA((2,)),
         ],
         compiler_params=pltpu.CompilerParams(
-            collective_id=0, has_side_effects=True, vmem_limit_bytes=32 * 1024 * 1024
+            collective_id=0, has_side_effects=True, vmem_limit_bytes=56 * 1024 * 1024
         ),
         cost_estimate=pl.CostEstimate(flops=3_000_000_000, bytes_accessed=700_000, transcendentals=0),
     )(
         right_side, initial_guess, point_cell, point_offset,
-        point_weight.reshape(16, 128), point_mask.reshape(16, 128), block_count,
+        point_weight.reshape(POINTS // COLS, COLS), point_mask.reshape(POINTS // COLS, COLS), block_count,
     )
 
 

time: 43 us -> 35.6 us (0.83)
  local copies, waits for them, and re-layouts: 6.02 us -> 2.26 us
  Pallas kernels: 35.4 us -> 31.9 us
    unnamed x14 -> x4, local copies, waits for them, and re-layouts: 6.02 us -> 2.26 us
    pallas_call x1, Pallas kernels: 35.4 us -> 31.9 us  [body(): pl.pallas_call(kernel, out_shape=(slab, slab), in_specs=[pl.BlockSpec(mem...]
where the time goes in v2:
time: 35.6 us; the launch traced here: 35.5 us
  Pallas kernels  31.9 us (90%)
  local copies, waits for them, and re-layouts  2.26 us (6%)
  between operations  1.3 us (4%)
    pallas_call x1, Pallas kernels, body(): pl.pallas_call(kernel, out_shape=(slab, slab), in_specs=[pl.BlockSpec(mem...  31.9 us
    unnamed x4, local copies, waits for them, and re-layouts  2.26 us

profile of v2, /device:TPU:1, one launch (start us, length us, event | category | flops | bytes accessed | tf_op | source)
XLA Modules:
  0.0 35.5 jit_solution(9376264466540038488)
XLA Ops:
  1.3 31.9 %shard_map.86 = (f32[4,64,128]{2,1,0:T(8,128)}, f32[4,64,128]{2,1,0:T(8,128)}) custom-call(f32[4,64,128]{2,1,0:T(8,128)} %right_in.1, f32[4,64,128]{2,1,0:T(8,128)} %guess_in.1, s32[3,2048]{1,0:T(4,128)} %cell_in.1, f32[3,2048]{1,0:T(4,128)} %offset_in.1, f32[16,128]{1,0:T(8,128)} %bitcast.2, s32[16,128]{1,0:T(8,128)} %bitcast.3, s32[1]{0:T(128)S(6)} %copy.11.count_ref), custom_call_target="tpu_custom_call" | custom-call | flops 3000000000 | bytes 700000 | tf_op jit(solution)/shard_map/pallas_call | solution.py:350
  33.2 0.0 copy-start
  33.2 1.6 %copy.12 = f32[4,64,128]{2,1,0:T(8,128)} copy(f32[4,64,128]{2,1,0:T(8,128)} %get-tuple-element.4) | data formatting | bytes 262144
  34.8 0.0 copy-done
  34.8 0.7 %copy.13 = f32[4,64,128]{2,1,0:T(8,128)} copy(f32[4,64,128]{2,1,0:T(8,128)S(1)} %copy-done) | data formatting | bytes 262144
Async XLA Ops:
  33.2 1.6 %copy-start = (f32[4,64,128]{2,1,0:T(8,128)S(1)}, f32[4,64,128]{2,1,0:T(8,128)}, u32[]{:S(2)}) copy-start(f32[4,64,128]{2,1,0:T(8,128)} %get-tuple-element.5) | copy-start | bytes 393220

commit v3 on v2

--- a/solution.py
+++ b/solution.py
@@ -178,12 +178,11 @@
 
 def kernel(
     right_in, guess_in, cell_in, offset_in, weight_in, mask_in, count_ref,
-    out_field, out_residual,
+    out_residual, out_image, out_second, out_factor,
     right_ref, cell_ref, offset_ref, weight_ref, mask_ref,
     guess, known, residual, image, second, stiff_ref, mass_ref,
     table_z, table_y, table_x, strength_ref, left_ref, spread_ref,
-    sums, arrived_a, arrived_b,
-    load_sem, halo_send, halo_recv, sum_send, sum_recv,
+    load_sem, halo_send, halo_recv, sum_send, sum_recv, sums, *arrivals,
 ):
     loads = [
         pltpu.make_async_copy(source, target, load_sem.at[k])
@@ -289,6 +288,9 @@
     def fold(value):
         return value.reshape(CELLS // 8, 8, COLS)
 
+    out_residual[...] = residual[2:6]
+    out_image[...] = image[2:6]
+    out_second[...] = second[...]
     r0 = fold(residual[2:6])
     scale = jnp.max(jnp.max(jnp.abs(r0), axis=0), axis=0, keepdims=True)
     scale = jnp.maximum(jnp.max(scale, axis=1, keepdims=True), 1e-30)
@@ -301,7 +303,7 @@
     ]
     row = packed(moments, scale)
 
-    for turn, arrived in enumerate((arrived_a, arrived_b)):
+    for turn, arrived in enumerate(arrivals):
         count = len(peers[turn])
         sums[turn] = row
         arrived[count : count + 1, :] = row
@@ -327,19 +329,17 @@
     a1 = (g - 1.0) * m1 / (a0 * m3 - g * m2)
     c1 = a0 + a1 * g
     c2 = a1 * a0
-    for k in range(PLANES):
-        out_field[k] = guess[4 + k] + c1 * residual[2 + k] - c2 * image[2 + k]
-        out_residual[k] = residual[2 + k] - c1 * image[2 + k] + c2 * second[k]
+    out_factor[...] = jnp.concatenate([jnp.broadcast_to(c, (1, COLS)) for c in (c1, c2)] * 4, axis=0)
 
     for copy in started:
         copy.wait_send()
-    for turn, arrived in enumerate((arrived_a, arrived_b)):
+    for turn, arrived in enumerate(arrivals):
         whole = arrived.at[pl.ds(0, len(peers[turn]))]
         pltpu.make_async_copy(whole, whole, sum_send.at[turn]).wait()
 
 
 def body(right_side, initial_guess, point_cell, point_offset, point_weight, point_mask, block_count):
-    slab = jax.ShapeDtypeStruct((PLANES, ROWS, COLS), jnp.float32)
+    slab = pltpu.VMEM((PLANES, ROWS, COLS), jnp.float32)
     vmem = pl.BlockSpec(memory_space=pltpu.VMEM)
     groups = []
     for axes in STAGES:
@@ -347,11 +347,11 @@
         for axis in axes:
             size *= SIZES[axis]
         groups.append(size)
-    return pl.pallas_call(
+    r0, w, u, factor = pl.pallas_call(
         kernel,
-        out_shape=(slab, slab),
+        out_shape=(slab, slab, slab, pltpu.VMEM((8, COLS), jnp.float32)),
         in_specs=[pl.BlockSpec(memory_space=pltpu.HBM)] * 6 + [pl.BlockSpec(memory_space=pltpu.SMEM)],
-        out_specs=(vmem, vmem),
+        out_specs=(vmem,) * 4,
         scratch_shapes=[
             pltpu.VMEM((PLANES, ROWS, COLS), jnp.float32),
             pltpu.VMEM((3, POINTS), jnp.int32),
@@ -371,15 +371,14 @@
             pltpu.VMEM((8, POINTS), jnp.float32),
             pltpu.VMEM((2 * CELLS, 2 * COLS), jnp.bfloat16),
             pltpu.VMEM((2 * CELLS, POINTS), jnp.bfloat16),
-            pltpu.VMEM((2, 1, COLS), jnp.float32),
-            pltpu.VMEM((groups[0], COLS), jnp.float32),
-            pltpu.VMEM((groups[1], COLS), jnp.float32),
             pltpu.SemaphoreType.DMA((6,)),
             pltpu.SemaphoreType.DMA((4, 2)),
             pltpu.SemaphoreType.DMA((4, 2)),
-            pltpu.SemaphoreType.DMA((2,)),
-            pltpu.SemaphoreType.DMA((2,)),
-        ],
+            pltpu.SemaphoreType.DMA((len(STAGES),)),
+            pltpu.SemaphoreType.DMA((len(STAGES),)),
+            pltpu.VMEM((len(STAGES), 1, COLS), jnp.float32),
+        ]
+        + [pltpu.VMEM((size, COLS), jnp.float32) for size in groups],
         compiler_params=pltpu.CompilerParams(
             collective_id=0, has_side_effects=True, vmem_limit_bytes=56 * 1024 * 1024
         ),
@@ -388,6 +387,8 @@
         right_side, initial_guess, point_cell, point_offset,
         point_weight.reshape(POINTS // COLS, COLS), point_mask.reshape(POINTS // COLS, COLS), block_count,
     )
+    c1, c2 = factor[0], factor[1]
+    return initial_guess + c1 * r0 - c2 * w, r0 - c1 * w + c2 * u
 
 
 def solution(mesh):

time: 35.6 us -> 33.4 us (0.938)
  local copies, waits for them, and re-layouts: 2.26 us -> 0.01 us
  other arithmetic: 0 us -> 0.75 us
  Pallas kernels: 31.9 us -> 31.2 us
    unnamed x4 -> x2, local copies, waits for them, and re-layouts: 2.26 us -> 0.01 us
    add x0 -> x1, other arithmetic: none -> 0.75 us  [body(): return (initial_guess + c1 * r0 - c2 * w, r0 - c1 * w + c2 * u)]
    pallas_call x1, Pallas kernels: 31.9 us -> 31.2 us  [body(): pl.pallas_call(kernel, out_shape=(slab, slab, slab, pltpu.VMEM((8, COLS),...]
where the time goes in v3:
time: 33.4 us; the launch traced here: 33.3 us
  Pallas kernels  31.2 us (93%)
  between operations  1.31 us (4%)
  other arithmetic  0.75 us (2%)
    pallas_call x1, Pallas kernels, body(): pl.pallas_call(kernel, out_shape=(slab, slab, slab, pltpu.VMEM((8, COLS),...  31.2 us
    add x1, other arithmetic, body(): return (initial_guess + c1 * r0 - c2 * w, r0 - c1 * w + c2 * u)  0.75 us

profile of v3, /device:TPU:1, one launch (start us, length us, event | category | flops | bytes accessed | tf_op | source)
XLA Modules:
  0.0 33.3 jit_solution(6198161094973979288)
XLA Ops:
  1.3 0.0 copy-start
  1.3 31.2 %shard_map.86 = (f32[4,64,128]{2,1,0:T(8,128)S(1)}, f32[4,64,128]{2,1,0:T(8,128)S(1)}, f32[4,64,128]{2,1,0:T(8,128)S(1)}, f32[8,128]{1,0:T(8,128)S(1)}) custom-call(f32[4,64,128]{2,1,0:T(8,128)} %right_in.1, f32[4,64,128]{2,1,0:T(8,128)} %guess_in.1, s32[3,2048]{1,0:T(4,128)} %cell_in.1, f32[3,2048]{1,0:T(4,128)} %offset_in.1, f32[16,128]{1,0:T(8,128)} %bitcast.6, ...), custom_call_target="tpu_custom_call" | custom-call | flops 3000000000 | bytes 700000 | tf_op jit(solution)/shard_map/pallas_call | solution.py:350
  32.5 0.0 copy-done
  32.5 0.7 %multiply_add_fusion = (f32[4,64,128]{2,1,0:T(8,128)}, f32[4,64,128]{2,1,0:T(8,128)}) fusion(f32[4,64,128]{2,1,0:T(8,128)S(1)} %get-tuple-element.9, f32[4,64,128]{2,1,0:T(8,128)S(1)} %get-tuple-element.7, f32[4,64,128]{2,1,0:T(8,128)S(1)} %get-tuple-element.8, f32[128]{0:T(128)S(1)} %get-tuple-element.13, f32[128]{0:T(128)S(1)} %get-tuple-element.12, ...), kind=kLoop, calls=%fused_computation | loop fusion | flops 262144 | bytes 787456 | tf_op jit(solution)/shard_map/add | solution.py:391
  (1 shorter events, 0.0 us)
Async XLA Ops:
  1.3 31.2 %copy-start = (f32[4,64,128]{2,1,0:T(8,128)S(1)}, f32[4,64,128]{2,1,0:T(8,128)}, u32[]{:S(2)}) copy-start(f32[4,64,128]{2,1,0:T(8,128)} %guess_in.1) | copy-start | bytes 393220

commit v4 on v3

--- a/solution.py
+++ b/solution.py
@@ -125,19 +125,38 @@
     return result[:, 0:COLS] + result[:, COLS : 2 * COLS]
 
 
-def mass(values):
-    return (66.0 / 120.0) * values[2] + (26.0 / 120.0) * (values[1] + values[3]) + (1.0 / 120.0) * (values[0] + values[4])
-
-
-def stiff(values):
-    return values[2] - (1.0 / 3.0) * (values[1] + values[3]) - (1.0 / 6.0) * (values[0] + values[4])
-
-
-def stencil(planes, stiff_ref, mass_ref):
-    count = len(planes) - 4
-    for k in range(count):
-        stiff_ref[k, EDGE : EDGE + ROWS, :] = stiff(planes[k : k + 5])
-        mass_ref[k, EDGE : EDGE + ROWS, :] = mass(planes[k : k + 5])
+MASS_TAPS = (1.0 / 120.0, 26.0 / 120.0, 66.0 / 120.0)
+STIFF_TAPS = (-1.0 / 6.0, -1.0 / 3.0, 1.0)
+
+
+def five(taps, values):
+    return taps[2] * values[2] + taps[1] * (values[1] + values[3]) + taps[0] * (values[0] + values[4])
+
+
+def own_part(taps, p):
+    near, far = taps[1], taps[0]
+    return [
+        taps[2] * p[0] + near * p[1] + far * p[2],
+        taps[2] * p[1] + near * (p[0] + p[2]) + far * p[3],
+        taps[2] * p[2] + near * (p[1] + p[3]) + far * p[0],
+        taps[2] * p[3] + near * p[2] + far * p[1],
+    ]
+
+
+def cross_part(taps, p):
+    near, far = taps[1], taps[0]
+    return [far * p[0] + near * p[1], far * p[1], far * p[2], near * p[2] + far * p[3]]
+
+
+def outward_part(taps, p):
+    near, far = taps[1], taps[0]
+    return [far * p[0], near * p[0] + far * p[1], far * p[2] + near * p[3], far * p[3]]
+
+
+def stencil(part, planes, stiff_ref, mass_ref):
+    for k, (stiff_x, mass_x) in enumerate(zip(part(STIFF_TAPS, planes), part(MASS_TAPS, planes))):
+        stiff_ref[k, EDGE : EDGE + ROWS, :] = stiff_x
+        mass_ref[k, EDGE : EDGE + ROWS, :] = mass_x
     lane = lax.broadcasted_iota(jnp.int32, (ROWS, COLS), 1)
 
     def along_z(value):
@@ -150,10 +169,11 @@
         ]
 
     out = []
-    for k in range(count):
+    for k in range(PLANES):
         stiff_x = [stiff_ref[k, EDGE - 2 + s : EDGE - 2 + s + ROWS, :] for s in range(5)]
         mass_x = [mass_ref[k, EDGE - 2 + s : EDGE - 2 + s + ROWS, :] for s in range(5)]
-        out.append(mass(along_z(mass(stiff_x) + stiff(mass_x))) + stiff(along_z(mass(mass_x))))
+        mixed = five(MASS_TAPS, stiff_x) + five(STIFF_TAPS, mass_x)
+        out.append(five(MASS_TAPS, along_z(mixed)) + five(STIFF_TAPS, along_z(five(MASS_TAPS, mass_x))))
     return out
 
 
@@ -178,12 +198,22 @@
 
 def kernel(
     right_in, guess_in, cell_in, offset_in, weight_in, mask_in, count_ref,
-    out_residual, out_image, out_second, out_factor,
+    residual, image, second, out_factor,
     right_ref, cell_ref, offset_ref, weight_ref, mask_ref,
-    guess, known, residual, image, second, stiff_ref, mass_ref,
+    guess, known, partial, outward, stiff_ref, mass_ref,
     table_z, table_y, table_x, strength_ref, left_ref, spread_ref,
     load_sem, halo_send, halo_recv, sum_send, sum_recv, sums, *arrivals,
 ):
+    here = coordinates()
+    device = lax.axis_index("bricks") * 4 + lax.axis_index("pts")
+    before, after = (device + 255) % 256, (device + 1) % 256
+    left, right = (before // 4, before % 4), (after // 4, after % 4)
+    peers = [stage_peers(here, axes) for axes in STAGES]
+
+    barrier = pltpu.get_barrier_semaphore()
+    greeted = [left, right] + [p for stage in peers for p in stage]
+    for peer in greeted[0:2]:
+        pl.semaphore_signal(barrier, inc=1, device_id=peer, device_id_type=MESH)
     loads = [
         pltpu.make_async_copy(source, target, load_sem.at[k])
         for k, (source, target) in enumerate((
@@ -191,22 +221,13 @@
             (offset_in, offset_ref),
             (weight_in, weight_ref),
             (mask_in, mask_ref),
-            (guess_in, guess.at[pl.ds(4, PLANES)]),
+            (guess_in, guess.at[pl.ds(2, PLANES)]),
             (right_in, right_ref),
         ))
     ]
     for load in loads:
         load.start()
-
-    here = coordinates()
-    device = lax.axis_index("bricks") * 4 + lax.axis_index("pts")
-    before, after = (device + 255) % 256, (device + 1) % 256
-    left, right = (before // 4, before % 4), (after // 4, after % 4)
-    peers = [stage_peers(here, axes) for axes in STAGES]
-
-    barrier = pltpu.get_barrier_semaphore()
-    greeted = [left, right] + [p for stage in peers for p in stage]
-    for peer in greeted:
+    for peer in greeted[2:]:
         pl.semaphore_signal(barrier, inc=1, device_id=peer, device_id_type=MESH)
 
     first, last = device == 0, device == 255
@@ -222,9 +243,9 @@
     pl.semaphore_wait(barrier, len(greeted))
     started = []
 
-    def send(field, turn, moves):
+    def send(field, turn):
         copies = []
-        for side, (source, target) in enumerate(moves):
+        for side, (source, target) in enumerate(((2, 6), (4, 0))):
             copy = pltpu.make_async_remote_copy(
                 src_ref=field.at[pl.ds(source, 2)],
                 dst_ref=field.at[pl.ds(target, 2)],
@@ -245,62 +266,74 @@
     def screened(field):
         return screen(field.reshape(CELLS, COLS), *tables).reshape(PLANES, ROWS, COLS)
 
-    def outside(planes, side):
-        return [jnp.where(side, 0.0, p) for p in planes]
-
-    near = send(guess, 0, ((4, 8), (6, 2)))
-    far = send(guess, 1, ((6, 10), (4, 0)))
-    value = screened(guess[4:8])
-    loads[5].wait()
-    known[2:6] = right_ref[...] - value
-    edge = send(known, 2, ((2, 6), (4, 0)))
-
-    landed(near)
-    planes = outside([guess[k] for k in (2, 3)], first) + [guess[k] for k in range(4, 8)]
-    planes = planes + outside([guess[k] for k in (8, 9)], last)
-    smooth = stencil(planes, stiff_ref, mass_ref)
-    for k in range(PLANES):
-        residual[2 + k] = known[2 + k] - smooth[k]
-    second[...] = screened(residual[2:6])
-
-    landed(far)
-    landed(edge)
-    smooth = stencil([guess[k] for k in range(0, 6)], stiff_ref, mass_ref)
-    for k in range(2):
-        residual[k] = jnp.where(first, 0.0, known[k] - smooth[k])
-    smooth = stencil([guess[k] for k in range(6, 12)], stiff_ref, mass_ref)
-    for k in range(2):
-        residual[6 + k] = jnp.where(last, 0.0, known[6 + k] - smooth[k])
-    smooth = stencil([residual[k] for k in range(8)], stiff_ref, mass_ref)
-    for k in range(PLANES):
-        image[2 + k] = smooth[k] + second[k]
-    edge = send(image, 3, ((2, 6), (4, 0)))
-
-    value = screened(image[2:6])
-    second[...] = value
-    landed(edge)
-    planes = outside([image[k] for k in (0, 1)], first) + [image[k] for k in range(2, 6)]
-    planes = planes + outside([image[k] for k in (6, 7)], last)
-    smooth = stencil(planes, stiff_ref, mass_ref)
-    for k in range(PLANES):
-        second[k] = second[k] + smooth[k]
+    def smooth(part, planes):
+        return stencil(part, planes, stiff_ref, mass_ref)
+
+    def four(ref, at):
+        return [ref[at + k] for k in range(PLANES)]
+
+    def beside(field, added):
+        planes = [field[k] for k in (0, 1, 6, 7)]
+        if added is not None:
+            planes = [p + outward[k] for k, p in enumerate(planes)]
+        return [jnp.where(first, 0.0, p) for p in planes[0:2]] + [jnp.where(last, 0.0, p) for p in planes[2:4]]
 
     def fold(value):
         return value.reshape(CELLS // 8, 8, COLS)
 
-    out_residual[...] = residual[2:6]
-    out_image[...] = image[2:6]
-    out_second[...] = second[...]
-    r0 = fold(residual[2:6])
-    scale = jnp.max(jnp.max(jnp.abs(r0), axis=0), axis=0, keepdims=True)
+    def dot(a, b):
+        return jnp.sum(fold(a) * fold(b), axis=0)
+
+    copies = send(guess, 0)
+    own = smooth(own_part, four(guess, 2))
+    loads[5].wait()
+    for k in range(PLANES):
+        known[2 + k] = right_ref[k] - own[k]
+    known[2:6] = known[2:6] - screened(guess[2:6])
+    edge = send(known, 1)
+    added = smooth(outward_part, four(guess, 2))
+    for k in range(PLANES):
+        outward[k] = -added[k]
+
+    landed(copies)
+    added = smooth(cross_part, beside(guess, None))
+    for k in range(PLANES):
+        residual[k] = known[2 + k] - added[k]
+    own = smooth(own_part, four(residual, 0))
+    for k in range(PLANES):
+        partial[2 + k] = own[k]
+    partial[2:6] = partial[2:6] + screened(residual[...])
+    copies = send(partial, 2)
+
+    landed(edge)
+    added = smooth(cross_part, beside(known, outward))
+    for k in range(PLANES):
+        image[k] = partial[2 + k] + added[k]
+    added = smooth(outward_part, four(residual, 0))
+    for k in range(PLANES):
+        outward[k] = added[k]
+    own = smooth(own_part, four(image, 0))
+    for k in range(PLANES):
+        second[k] = own[k]
+    second[...] = second[...] + screened(image[...])
+
+    scale = jnp.max(jnp.max(jnp.abs(fold(residual[...])), axis=0), axis=0, keepdims=True)
     scale = jnp.maximum(jnp.max(scale, axis=1, keepdims=True), 1e-30)
     inverse = 1.0 / scale
-    r0 = r0 * inverse
-    w = fold(image[2:6]) * inverse
-    u = fold(second[...]) * inverse
-    moments = [
-        jnp.sum(jnp.sum(a * b, axis=0), axis=0, keepdims=True) for a, b in ((r0, r0), (r0, w), (w, w), (w, u))
-    ]
+    r0 = residual[...] * inverse
+    w = image[...] * inverse
+    u = second[...] * inverse
+    moments = [dot(r0, r0), dot(r0, w), dot(w, w)]
+    last_moment = dot(w, u)
+
+    landed(copies)
+    added = smooth(cross_part, beside(partial, outward))
+    for k in range(PLANES):
+        second[k] = second[k] + added[k]
+        last_moment = last_moment + jnp.sum(
+            ((image[k] * inverse) * (added[k] * inverse)).reshape(ROWS // 8, 8, COLS), axis=0
+        )
+    moments = [jnp.sum(m, axis=0, keepdims=True) for m in moments + [last_moment]]
     row = packed(moments, scale)
 
     for turn, arrived in enumerate(arrivals):
@@ -358,7 +391,6 @@
             pltpu.VMEM((3, POINTS), jnp.float32),
             pltpu.VMEM((POINTS // COLS, COLS), jnp.float32),
             pltpu.VMEM((POINTS // COLS, COLS), jnp.int32),
-            pltpu.VMEM((PLANES + 8, ROWS, COLS), jnp.float32),
             pltpu.VMEM((PLANES + 4, ROWS, COLS), jnp.float32),
             pltpu.VMEM((PLANES + 4, ROWS, COLS), jnp.float32),
             pltpu.VMEM((PLANES + 4, ROWS, COLS), jnp.float32),
@@ -372,8 +404,8 @@
             pltpu.VMEM((2 * CELLS, 2 * COLS), jnp.bfloat16),
             pltpu.VMEM((2 * CELLS, POINTS), jnp.bfloat16),
             pltpu.SemaphoreType.DMA((6,)),
-            pltpu.SemaphoreType.DMA((4, 2)),
-            pltpu.SemaphoreType.DMA((4, 2)),
+            pltpu.SemaphoreType.DMA((3, 2)),
+            pltpu.SemaphoreType.DMA((3, 2)),
             pltpu.SemaphoreType.DMA((len(STAGES),)),
             pltpu.SemaphoreType.DMA((len(STAGES),)),
             pltpu.VMEM((len(STAGES), 1, COLS), jnp.float32),

time: 33.4 us -> 32.2 us (0.964)
  Pallas kernels: 31.2 us -> 30 us
    pallas_call x1, Pallas kernels: 31.2 us -> 30 us  [body(): pl.pallas_call(kernel, out_shape=(slab, slab, slab, pltpu.VMEM((8, COLS),...]
where the time goes in v4:
time: 32.2 us; the launch traced here: 32.1 us
  Pallas kernels  30 us (93%)
  between operations  1.31 us (4%)
  other arithmetic  0.75 us (2%)
    pallas_call x1, Pallas kernels, body(): pl.pallas_call(kernel, out_shape=(slab, slab, slab, pltpu.VMEM((8, COLS),...  30 us
    add x1, other arithmetic, body(): return (initial_guess + c1 * r0 - c2 * w, r0 - c1 * w + c2 * u)  0.75 us

profile of v4, /device:TPU:1, one launch (start us, length us, event | category | flops | bytes accessed | tf_op | source)
XLA Modules:
  0.0 32.1 jit_solution(3614544528806963103)
XLA Ops:
  1.3 0.0 copy-start
  1.3 30.0 %shard_map.86 = (f32[4,64,128]{2,1,0:T(8,128)S(1)}, f32[4,64,128]{2,1,0:T(8,128)S(1)}, f32[4,64,128]{2,1,0:T(8,128)S(1)}, f32[8,128]{1,0:T(8,128)S(1)}) custom-call(f32[4,64,128]{2,1,0:T(8,128)} %right_in.1, f32[4,64,128]{2,1,0:T(8,128)} %guess_in.1, s32[3,2048]{1,0:T(4,128)} %cell_in.1, f32[3,2048]{1,0:T(4,128)} %offset_in.1, f32[16,128]{1,0:T(8,128)} %bitcast.6, ...), custom_call_target="tpu_custom_call" | custom-call | flops 3000000000 | bytes 700000 | tf_op jit(solution)/shard_map/pallas_call | solution.py:383
  31.3 0.0 copy-done
  31.3 0.7 %multiply_add_fusion = (f32[4,64,128]{2,1,0:T(8,128)}, f32[4,64,128]{2,1,0:T(8,128)}) fusion(f32[4,64,128]{2,1,0:T(8,128)S(1)} %get-tuple-element.9, f32[4,64,128]{2,1,0:T(8,128)S(1)} %get-tuple-element.7, f32[4,64,128]{2,1,0:T(8,128)S(1)} %get-tuple-element.8, f32[128]{0:T(128)S(1)} %get-tuple-element.13, f32[128]{0:T(128)S(1)} %get-tuple-element.12, ...), kind=kLoop, calls=%fused_computation | loop fusion | flops 262144 | bytes 787456 | tf_op jit(solution)/shard_map/add | solution.py:423
  (1 shorter events, 0.0 us)
Async XLA Ops:
  1.3 30.1 %copy-start = (f32[4,64,128]{2,1,0:T(8,128)S(1)}, f32[4,64,128]{2,1,0:T(8,128)}, u32[]{:S(2)}) copy-start(f32[4,64,128]{2,1,0:T(8,128)} %guess_in.1) | copy-start | bytes 393220

commit v5 on v4

--- a/solution.py
+++ b/solution.py
@@ -19,7 +19,9 @@
 EDGE = 8
 
 SIZES = {"x": 4, "y": 4, "z": 8, "core": 2}
-STAGES = (("x", "y", "core"), ("z",))
+STAGES = (("core",), ("x", "y", "z"))
+GREETED = ("y", "z")
+TOLD = ("x", "core")
 
 
 def spline_weights(offset):
@@ -45,7 +47,8 @@
     for axis in axes:
         steps = [dict(step, **{axis: k}) for step in steps for k in range(SIZES[axis])]
     peers = []
-    for step in steps[1:]:
+    far = lambda step: sum(min(k, SIZES[axis] - k) for axis, k in step.items())
+    for step in sorted(steps[1:], key=far, reverse=True):
         place = dict(here)
         for axis, k in step.items():
             if k:
@@ -65,7 +68,7 @@
 
 
 def build_tables(cell_ref, offset_ref, weight_ref, mask_ref, count_ref, table_z, table_y, table_x, strength_ref):
-    count = count_ref[0]
+    count = count_ref[0:1, 0:1]
     for block in range(BLOCKS):
         lanes = pl.ds(block * BLOCK, BLOCK)
 
@@ -177,23 +180,25 @@
     return out
 
 
-def packed(moments, scale):
+def folded(moment, lanes):
+    shift = COLS // 2
+    while shift >= lanes:
+        moment = moment + pltpu.roll(moment, shift, 1)
+        shift //= 2
+    return moment
+
+
+def lane_groups():
     lane = lax.broadcasted_iota(jnp.int32, (1, COLS), 1)
-    row = jnp.broadcast_to(scale, (1, COLS))
-    for k, moment in enumerate(moments):
-        for shift in (64, 32, 16):
-            moment = moment + pltpu.roll(moment, shift, 1)
-        row = jnp.where(lane // 16 == k, moment, row)
-    return row
+    return [lane // 8 == 4, lane // 8 == 5, lane // 8 == 6, lane < 32]
 
 
 def combine(rows):
-    lane = lax.broadcasted_iota(jnp.int32, rows.shape, 1)
-    scales = jnp.max(jnp.where(lane >= 64, rows, 0.0), axis=1, keepdims=True)
-    largest = jnp.max(scales, axis=0, keepdims=True)
-    ratio = scales / largest
+    lane = lax.broadcasted_iota(jnp.int32, (1, COLS), 1)
+    largest = jnp.max(rows, axis=0, keepdims=True)
+    ratio = pltpu.roll(rows * (1.0 / largest), COLS // 2, 1)
     total = jnp.sum(rows * (ratio * ratio), axis=0, keepdims=True)
-    return jnp.where(lane[0:1] >= 64, largest, total)
+    return jnp.where(lane >= 64, largest, total)
 
 
 def kernel(
@@ -202,7 +207,7 @@
     right_ref, cell_ref, offset_ref, weight_ref, mask_ref,
     guess, known, partial, outward, stiff_ref, mass_ref,
     table_z, table_y, table_x, strength_ref, left_ref, spread_ref,
-    load_sem, halo_send, halo_recv, sum_send, sum_recv, sums, *arrivals,
+    load_sem, halo_send, halo_recv, sum_send, sum_recv, entered, sums, *arrivals,
 ):
     here = coordinates()
     device = lax.axis_index("bricks") * 4 + lax.axis_index("pts")
@@ -211,7 +216,8 @@
     peers = [stage_peers(here, axes) for axes in STAGES]
 
     barrier = pltpu.get_barrier_semaphore()
-    greeted = [left, right] + [p for stage in peers for p in stage]
+    told = stage_peers(here, TOLD)
+    greeted = [left, right] + stage_peers(here, GREETED) + told
     for peer in greeted[0:2]:
         pl.semaphore_signal(barrier, inc=1, device_id=peer, device_id_type=MESH)
     loads = [
@@ -285,6 +291,8 @@
         return jnp.sum(fold(a) * fold(b), axis=0)
 
     copies = send(guess, 0)
+    for peer in told:
+        pl.semaphore_signal(entered, inc=1, device_id=peer, device_id_type=MESH)
     own = smooth(own_part, four(guess, 2))
     loads[5].wait()
     for k in range(PLANES):
@@ -323,7 +331,10 @@
     r0 = residual[...] * inverse
     w = image[...] * inverse
     u = second[...] * inverse
-    moments = [dot(r0, r0), dot(r0, w), dot(w, w)]
+    groups = lane_groups()
+    row = jnp.where(lax.broadcasted_iota(jnp.int32, (1, COLS), 1) >= 64, scale, 0.0)
+    for group, a, b in zip(groups, (r0, r0, w), (r0, w, w)):
+        row = jnp.where(group, folded(jnp.sum(dot(a, b), axis=0, keepdims=True), 8), row)
     last_moment = dot(w, u)
 
     landed(copies)
@@ -333,8 +344,8 @@
         last_moment = last_moment + jnp.sum(
             ((image[k] * inverse) * (added[k] * inverse)).reshape(ROWS // 8, 8, COLS), axis=0
         )
-    moments = [jnp.sum(m, axis=0, keepdims=True) for m in moments + [last_moment]]
-    row = packed(moments, scale)
+    row = jnp.where(groups[3], folded(jnp.sum(last_moment, axis=0, keepdims=True), 32), row)
+    pl.semaphore_wait(entered, len(told))
 
     for turn, arrived in enumerate(arrivals):
         count = len(peers[turn])
@@ -353,10 +364,7 @@
         pltpu.make_async_copy(whole, whole, sum_recv.at[turn]).wait()
         row = combine(arrived[...])
 
-    lane = lax.broadcasted_iota(jnp.int32, (1, COLS), 1)
-    m0, m1, m2, m3 = (
-        jnp.sum(jnp.where(lane // 16 == k, row, 0.0), axis=1, keepdims=True) for k in range(4)
-    )
+    m0, m1, m2, m3 = (jnp.sum(jnp.where(group, row, 0.0), axis=1, keepdims=True) for group in groups)
     a0 = m0 / m1
     g = a0 * (m2 / m1)
     a1 = (g - 1.0) * m1 / (a0 * m3 - g * m2)
@@ -383,7 +391,7 @@
     r0, w, u, factor = pl.pallas_call(
         kernel,
         out_shape=(slab, slab, slab, pltpu.VMEM((8, COLS), jnp.float32)),
-        in_specs=[pl.BlockSpec(memory_space=pltpu.HBM)] * 6 + [pl.BlockSpec(memory_space=pltpu.SMEM)],
+        in_specs=[pl.BlockSpec(memory_space=pltpu.HBM)] * 6 + [vmem],
         out_specs=(vmem,) * 4,
         scratch_shapes=[
             pltpu.VMEM((PLANES, ROWS, COLS), jnp.float32),
@@ -408,6 +416,7 @@
             pltpu.SemaphoreType.DMA((3, 2)),
             pltpu.SemaphoreType.DMA((len(STAGES),)),
             pltpu.SemaphoreType.DMA((len(STAGES),)),
+            pltpu.SemaphoreType.REGULAR,
             pltpu.VMEM((len(STAGES), 1, COLS), jnp.float32),
         ]
         + [pltpu.VMEM((size, COLS), jnp.float32) for size in groups],
@@ -417,7 +426,7 @@
         cost_estimate=pl.CostEstimate(flops=3_000_000_000, bytes_accessed=700_000, transcendentals=0),
     )(
         right_side, initial_guess, point_cell, point_offset,
-        point_weight.reshape(POINTS // COLS, COLS), point_mask.reshape(POINTS // COLS, COLS), block_count,
+        point_weight.reshape(POINTS // COLS, COLS), point_mask.reshape(POINTS // COLS, COLS), block_count.reshape(1, 1),
     )
     c1, c2 = factor[0], factor[1]
     return initial_guess + c1 * r0 - c2 * w, r0 - c1 * w + c2 * u

time: 32.2 us -> 31.3 us (0.972)
  Pallas kernels: 30 us -> 29.1 us
    pallas_call x1, Pallas kernels: 30 us -> 29.1 us  [body(): pl.pallas_call(kernel, out_shape=(slab, slab, slab, pltpu.VMEM((8, COLS),...]
where the time goes in v5:
time: 31.3 us; the launch traced here: 31.2 us
  Pallas kernels  29.1 us (93%)
  between operations  1.31 us (4%)
  other arithmetic  0.75 us (2%)
    pallas_call x1, Pallas kernels, body(): pl.pallas_call(kernel, out_shape=(slab, slab, slab, pltpu.VMEM((8, COLS),...  29.1 us
    add x1, other arithmetic, body(): return (initial_guess + c1 * r0 - c2 * w, r0 - c1 * w + c2 * u)  0.75 us

profile of v5, /device:TPU:1, one launch (start us, length us, event | category | flops | bytes accessed | tf_op | source)
XLA Modules:
  0.0 31.2 jit_solution(10674561715509865753)
XLA Ops:
  1.3 0.0 copy-start
  1.3 29.1 %shard_map.86 = (f32[4,64,128]{2,1,0:T(8,128)S(1)}, f32[4,64,128]{2,1,0:T(8,128)S(1)}, f32[4,64,128]{2,1,0:T(8,128)S(1)}, f32[8,128]{1,0:T(8,128)S(1)}) custom-call(f32[4,64,128]{2,1,0:T(8,128)} %right_in.1, f32[4,64,128]{2,1,0:T(8,128)} %guess_in.1, s32[3,2048]{1,0:T(4,128)} %cell_in.1, f32[3,2048]{1,0:T(4,128)} %offset_in.1, f32[16,128]{1,0:T(8,128)} %bitcast.8, ...), custom_call_target="tpu_custom_call" | custom-call | flops 3000000000 | bytes 700000 | tf_op jit(solution)/shard_map/pallas_call | solution.py:391
  30.4 0.0 copy-done
  30.4 0.7 %multiply_add_fusion = (f32[4,64,128]{2,1,0:T(8,128)}, f32[4,64,128]{2,1,0:T(8,128)}) fusion(f32[4,64,128]{2,1,0:T(8,128)S(1)} %get-tuple-element.9, f32[4,64,128]{2,1,0:T(8,128)S(1)} %get-tuple-element.7, f32[4,64,128]{2,1,0:T(8,128)S(1)} %get-tuple-element.8, f32[128]{0:T(128)S(1)} %get-tuple-element.13, f32[128]{0:T(128)S(1)} %get-tuple-element.12, ...), kind=kLoop, calls=%fused_computation | loop fusion | flops 262144 | bytes 787456 | tf_op jit(solution)/shard_map/add | solution.py:432
  (1 shorter events, 0.0 us)
Async XLA Ops:
  1.3 29.1 %copy-start = (f32[4,64,128]{2,1,0:T(8,128)S(1)}, f32[4,64,128]{2,1,0:T(8,128)}, u32[]{:S(2)}) copy-start(f32[4,64,128]{2,1,0:T(8,128)} %guess_in.1) | copy-start | bytes 393220

commit v6 on v5

--- a/solution.py
+++ b/solution.py
@@ -20,8 +20,6 @@
 
 SIZES = {"x": 4, "y": 4, "z": 8, "core": 2}
 STAGES = (("core",), ("x", "y", "z"))
-GREETED = ("y", "z")
-TOLD = ("x", "core")
 
 
 def spline_weights(offset):
@@ -205,7 +203,7 @@
     right_in, guess_in, cell_in, offset_in, weight_in, mask_in, count_ref,
     residual, image, second, out_factor,
     right_ref, cell_ref, offset_ref, weight_ref, mask_ref,
-    guess, known, partial, outward, stiff_ref, mass_ref,
+    guess, known, partial, outward, weighed, stiff_ref, mass_ref,
     table_z, table_y, table_x, strength_ref, left_ref, spread_ref,
     load_sem, halo_send, halo_recv, sum_send, sum_recv, entered, sums, *arrivals,
 ):
@@ -216,8 +214,8 @@
     peers = [stage_peers(here, axes) for axes in STAGES]
 
     barrier = pltpu.get_barrier_semaphore()
-    told = stage_peers(here, TOLD)
-    greeted = [left, right] + stage_peers(here, GREETED) + told
+    lines = {axis: stage_peers(here, (axis,)) for axis in SIZES}
+    greeted = [left, right] + lines["z"] + lines["y"] + lines["x"] + lines["core"]
     for peer in greeted[0:2]:
         pl.semaphore_signal(barrier, inc=1, device_id=peer, device_id_type=MESH)
     loads = [
@@ -291,8 +289,8 @@
         return jnp.sum(fold(a) * fold(b), axis=0)
 
     copies = send(guess, 0)
-    for peer in told:
-        pl.semaphore_signal(entered, inc=1, device_id=peer, device_id_type=MESH)
+    for peer in lines["y"]:
+        pl.semaphore_signal(entered.at[0], inc=1, device_id=peer, device_id_type=MESH)
     own = smooth(own_part, four(guess, 2))
     loads[5].wait()
     for k in range(PLANES):
@@ -312,6 +310,9 @@
         partial[2 + k] = own[k]
     partial[2:6] = partial[2:6] + screened(residual[...])
     copies = send(partial, 2)
+    pl.semaphore_wait(entered.at[0], len(lines["y"]))
+    for peer in lines["x"]:
+        pl.semaphore_signal(entered.at[1], inc=1, device_id=peer, device_id_type=MESH)
 
     landed(edge)
     added = smooth(cross_part, beside(known, outward))
@@ -337,15 +338,18 @@
         row = jnp.where(group, folded(jnp.sum(dot(a, b), axis=0, keepdims=True), 8), row)
     last_moment = dot(w, u)
 
+    added = smooth(outward_part, four(image, 0))
+    for k in range(PLANES):
+        weighed[k] = added[k] * inverse
+
     landed(copies)
-    added = smooth(cross_part, beside(partial, outward))
-    for k in range(PLANES):
-        second[k] = second[k] + added[k]
+    halo = beside(partial, outward)
+    for k in range(PLANES):
         last_moment = last_moment + jnp.sum(
-            ((image[k] * inverse) * (added[k] * inverse)).reshape(ROWS // 8, 8, COLS), axis=0
+            ((halo[k] * inverse) * weighed[k]).reshape(ROWS // 8, 8, COLS), axis=0
         )
     row = jnp.where(groups[3], folded(jnp.sum(last_moment, axis=0, keepdims=True), 32), row)
-    pl.semaphore_wait(entered, len(told))
+    pl.semaphore_wait(entered.at[1], len(lines["x"]))
 
     for turn, arrived in enumerate(arrivals):
         count = len(peers[turn])
@@ -360,6 +364,10 @@
                 device_id=peer,
                 device_id_type=MESH,
             ).start()
+        if turn == len(STAGES) - 1:
+            added = smooth(cross_part, beside(partial, outward))
+            for k in range(PLANES):
+                second[k] = second[k] + added[k]
         whole = arrived.at[pl.ds(0, count)]
         pltpu.make_async_copy(whole, whole, sum_recv.at[turn]).wait()
         row = combine(arrived[...])
@@ -403,6 +411,7 @@
             pltpu.VMEM((PLANES + 4, ROWS, COLS), jnp.float32),
             pltpu.VMEM((PLANES + 4, ROWS, COLS), jnp.float32),
             pltpu.VMEM((PLANES, ROWS, COLS), jnp.float32),
+            pltpu.VMEM((PLANES, ROWS, COLS), jnp.float32),
             pltpu.VMEM((PLANES, ROWS + 2 * EDGE, COLS), jnp.float32),
             pltpu.VMEM((PLANES, ROWS + 2 * EDGE, COLS), jnp.float32),
             pltpu.VMEM((2 * COLS, POINTS), jnp.bfloat16),
@@ -416,7 +425,7 @@
             pltpu.SemaphoreType.DMA((3, 2)),
             pltpu.SemaphoreType.DMA((len(STAGES),)),
             pltpu.SemaphoreType.DMA((len(STAGES),)),
-            pltpu.SemaphoreType.REGULAR,
+            pltpu.SemaphoreType.REGULAR((2,)),
             pltpu.VMEM((len(STAGES), 1, COLS), jnp.float32),
         ]
         + [pltpu.VMEM((size, COLS), jnp.float32) for size in groups],

time: 31.3 us -> 30.2 us (0.965)
  Pallas kernels: 29.1 us -> 28 us
    pallas_call x1, Pallas kernels: 29.1 us -> 28 us  [body(): pl.pallas_call(kernel, out_shape=(slab, slab, slab, pltpu.VMEM((8, COLS),...]
where the time goes in v6:
time: 30.2 us; the launch traced here: 30.1 us
  Pallas kernels  28 us (93%)
  between operations  1.31 us (4%)
  other arithmetic  0.75 us (2%)
    pallas_call x1, Pallas kernels, body(): pl.pallas_call(kernel, out_shape=(slab, slab, slab, pltpu.VMEM((8, COLS),...  28 us
    add x1, other arithmetic, body(): return (initial_guess + c1 * r0 - c2 * w, r0 - c1 * w + c2 * u)  0.75 us

profile of v6, /device:TPU:1, one launch (start us, length us, event | category | flops | bytes accessed | tf_op | source)
XLA Modules:
  0.0 30.1 jit_solution(7707524001837945943)
XLA Ops:
  1.3 0.0 copy-start
  1.3 28.0 %shard_map.86 = (f32[4,64,128]{2,1,0:T(8,128)S(1)}, f32[4,64,128]{2,1,0:T(8,128)S(1)}, f32[4,64,128]{2,1,0:T(8,128)S(1)}, f32[8,128]{1,0:T(8,128)S(1)}) custom-call(f32[4,64,128]{2,1,0:T(8,128)} %right_in.1, f32[4,64,128]{2,1,0:T(8,128)} %guess_in.1, s32[3,2048]{1,0:T(4,128)} %cell_in.1, f32[3,2048]{1,0:T(4,128)} %offset_in.1, f32[16,128]{1,0:T(8,128)} %bitcast.8, ...), custom_call_target="tpu_custom_call" | custom-call | flops 3000000000 | bytes 700000 | tf_op jit(solution)/shard_map/pallas_call | solution.py:399
  29.4 0.0 copy-done
  29.4 0.7 %multiply_add_fusion = (f32[4,64,128]{2,1,0:T(8,128)}, f32[4,64,128]{2,1,0:T(8,128)}) fusion(f32[4,64,128]{2,1,0:T(8,128)S(1)} %get-tuple-element.9, f32[4,64,128]{2,1,0:T(8,128)S(1)} %get-tuple-element.7, f32[4,64,128]{2,1,0:T(8,128)S(1)} %get-tuple-element.8, f32[128]{0:T(128)S(1)} %get-tuple-element.13, f32[128]{0:T(128)S(1)} %get-tuple-element.12, ...), kind=kLoop, calls=%fused_computation | loop fusion | flops 262144 | bytes 787456 | tf_op jit(solution)/shard_map/add | solution.py:441
  (1 shorter events, 0.0 us)
Async XLA Ops:
  1.3 28.1 %copy-start = (f32[4,64,128]{2,1,0:T(8,128)S(1)}, f32[4,64,128]{2,1,0:T(8,128)}, u32[]{:S(2)}) copy-start(f32[4,64,128]{2,1,0:T(8,128)} %guess_in.1) | copy-start | bytes 393220

commit v7 on v6

--- a/solution.py
+++ b/solution.py
@@ -98,7 +98,7 @@
         )
 
 
-def screen(field, table_z, table_y, table_x, strength_ref, left_ref, spread_ref):
+def sample(field, table_z, table_y, table_x, strength_ref, left_ref, spread_ref):
     high, low = two_terms(field)
     left_ref[0:CELLS, 0:COLS] = high
     left_ref[0:CELLS, COLS : 2 * COLS] = high
@@ -119,6 +119,9 @@
             high, low = two_terms(along_y * (along_x[plane : plane + 1] * values))
             spread_ref[plane * ROWS : (plane + 1) * ROWS, lanes] = high
             spread_ref[CELLS + plane * ROWS : CELLS + (plane + 1) * ROWS, lanes] = low
+
+
+def gathered(table_z, spread_ref):
     result = lax.dot_general(
         spread_ref[...], table_z[...], (((1,), (1,)), ((), ())), preferred_element_type=jnp.float32
     )
@@ -217,6 +220,8 @@
     lines = {axis: stage_peers(here, (axis,)) for axis in SIZES}
     greeted = [left, right] + lines["z"] + lines["y"] + lines["x"] + lines["core"]
     for peer in greeted[0:2]:
+        pl.semaphore_signal(barrier, inc=1, device_id=peer, device_id_type=MESH)
+    for peer in greeted[2:]:
         pl.semaphore_signal(barrier, inc=1, device_id=peer, device_id_type=MESH)
     loads = [
         pltpu.make_async_copy(source, target, load_sem.at[k])
@@ -231,18 +236,11 @@
     ]
     for load in loads:
         load.start()
-    for peer in greeted[2:]:
-        pl.semaphore_signal(barrier, inc=1, device_id=peer, device_id_type=MESH)
 
     first, last = device == 0, device == 255
     for ref in (stiff_ref, mass_ref):
         ref[:, 0:EDGE, :] = jnp.zeros((PLANES, EDGE, COLS), jnp.float32)
         ref[:, EDGE + ROWS : 2 * EDGE + ROWS, :] = jnp.zeros((PLANES, EDGE, COLS), jnp.float32)
-    for load in loads[0:4]:
-        load.wait()
-    build_tables(cell_ref, offset_ref, weight_ref, mask_ref, count_ref, table_z, table_y, table_x, strength_ref)
-    tables = (table_z, table_y, table_x, strength_ref, left_ref, spread_ref)
-
     loads[4].wait()
     pl.semaphore_wait(barrier, len(greeted))
     started = []
@@ -268,7 +266,8 @@
             copy.wait_recv()
 
     def screened(field):
-        return screen(field.reshape(CELLS, COLS), *tables).reshape(PLANES, ROWS, COLS)
+        sample(field.reshape(CELLS, COLS), *tables)
+        return gathered(table_z, spread_ref).reshape(PLANES, ROWS, COLS)
 
     def smooth(part, planes):
         return stencil(part, planes, stiff_ref, mass_ref)
@@ -291,6 +290,11 @@
     copies = send(guess, 0)
     for peer in lines["y"]:
         pl.semaphore_signal(entered.at[0], inc=1, device_id=peer, device_id_type=MESH)
+    for load in loads[0:4]:
+        load.wait()
+    build_tables(cell_ref, offset_ref, weight_ref, mask_ref, count_ref, table_z, table_y, table_x, strength_ref)
+    tables = (table_z, table_y, table_x, strength_ref, left_ref, spread_ref)
+
     own = smooth(own_part, four(guess, 2))
     loads[5].wait()
     for k in range(PLANES):
@@ -305,10 +309,11 @@
     added = smooth(cross_part, beside(guess, None))
     for k in range(PLANES):
         residual[k] = known[2 + k] - added[k]
+    sample(residual[...].reshape(CELLS, COLS), *tables)
+    spread = gathered(table_z, spread_ref)
     own = smooth(own_part, four(residual, 0))
     for k in range(PLANES):
-        partial[2 + k] = own[k]
-    partial[2:6] = partial[2:6] + screened(residual[...])
+        partial[2 + k] = own[k] + spread[k * ROWS : (k + 1) * ROWS]
     copies = send(partial, 2)
     pl.semaphore_wait(entered.at[0], len(lines["y"]))
     for peer in lines["x"]:

time: 30.2 us -> 30.2 us (level)
  no operation moved by 1% of the time
where the time goes in v7:
time: 30.2 us; the launch traced here: 30.1 us
  Pallas kernels  28 us (93%)
  between operations  1.31 us (4%)
  other arithmetic  0.75 us (2%)
    pallas_call x1, Pallas kernels, body(): pl.pallas_call(kernel, out_shape=(slab, slab, slab, pltpu.VMEM((8, COLS),...  28 us
    add x1, other arithmetic, body(): return (initial_guess + c1 * r0 - c2 * w, r0 - c1 * w + c2 * u)  0.75 us

profile of v7, /device:TPU:1, one launch (start us, length us, event | category | flops | bytes accessed | tf_op | source)
XLA Modules:
  0.0 30.1 jit_solution(13195124218764102970)
XLA Ops:
  1.3 0.0 copy-start
  1.3 28.0 %shard_map.86 = (f32[4,64,128]{2,1,0:T(8,128)S(1)}, f32[4,64,128]{2,1,0:T(8,128)S(1)}, f32[4,64,128]{2,1,0:T(8,128)S(1)}, f32[8,128]{1,0:T(8,128)S(1)}) custom-call(f32[4,64,128]{2,1,0:T(8,128)} %right_in.1, f32[4,64,128]{2,1,0:T(8,128)} %guess_in.1, s32[3,2048]{1,0:T(4,128)} %cell_in.1, f32[3,2048]{1,0:T(4,128)} %offset_in.1, f32[16,128]{1,0:T(8,128)} %bitcast.8, ...), custom_call_target="tpu_custom_call" | custom-call | flops 3000000000 | bytes 700000 | tf_op jit(solution)/shard_map/pallas_call | solution.py:404
  29.3 0.0 copy-done
  29.3 0.7 %multiply_add_fusion = (f32[4,64,128]{2,1,0:T(8,128)}, f32[4,64,128]{2,1,0:T(8,128)}) fusion(f32[4,64,128]{2,1,0:T(8,128)S(1)} %get-tuple-element.9, f32[4,64,128]{2,1,0:T(8,128)S(1)} %get-tuple-element.7, f32[4,64,128]{2,1,0:T(8,128)S(1)} %get-tuple-element.8, f32[128]{0:T(128)S(1)} %get-tuple-element.13, f32[128]{0:T(128)S(1)} %get-tuple-element.12, ...), kind=kLoop, calls=%fused_computation | loop fusion | flops 262144 | bytes 787456 | tf_op jit(solution)/shard_map/add | solution.py:446
  (1 shorter events, 0.0 us)
Async XLA Ops:
  1.3 28.1 %copy-start = (f32[4,64,128]{2,1,0:T(8,128)S(1)}, f32[4,64,128]{2,1,0:T(8,128)}, u32[]{:S(2)}) copy-start(f32[4,64,128]{2,1,0:T(8,128)} %guess_in.1) | copy-start | bytes 393220

commit v8 on v6

--- a/solution.py
+++ b/solution.py
@@ -201,7 +201,7 @@
 
 def kernel(
     right_in, guess_in, cell_in, offset_in, weight_in, mask_in, count_ref,
-    residual, image, second, out_factor,
+    residual, image, second, out_first, out_second,
     right_ref, cell_ref, offset_ref, weight_ref, mask_ref,
     guess, known, partial, outward, weighed, stiff_ref, mass_ref,
     table_z, table_y, table_x, strength_ref, left_ref, spread_ref,
@@ -378,7 +378,8 @@
     a1 = (g - 1.0) * m1 / (a0 * m3 - g * m2)
     c1 = a0 + a1 * g
     c2 = a1 * a0
-    out_factor[...] = jnp.concatenate([jnp.broadcast_to(c, (1, COLS)) for c in (c1, c2)] * 4, axis=0)
+    out_first[...] = jnp.broadcast_to(c1, (1, COLS))
+    out_second[...] = jnp.broadcast_to(c2, (1, COLS))
 
     for copy in started:
         copy.wait_send()
@@ -396,11 +397,11 @@
         for axis in axes:
             size *= SIZES[axis]
         groups.append(size)
-    r0, w, u, factor = pl.pallas_call(
+    r0, w, u, c1, c2 = pl.pallas_call(
         kernel,
-        out_shape=(slab, slab, slab, pltpu.VMEM((8, COLS), jnp.float32)),
+        out_shape=(slab, slab, slab) + (pltpu.VMEM((1, COLS), jnp.float32),) * 2,
         in_specs=[pl.BlockSpec(memory_space=pltpu.HBM)] * 6 + [vmem],
-        out_specs=(vmem,) * 4,
+        out_specs=(vmem,) * 5,
         scratch_shapes=[
             pltpu.VMEM((PLANES, ROWS, COLS), jnp.float32),
             pltpu.VMEM((3, POINTS), jnp.int32),
@@ -437,7 +438,6 @@
         right_side, initial_guess, point_cell, point_offset,
         point_weight.reshape(POINTS // COLS, COLS), point_mask.reshape(POINTS // COLS, COLS), block_count.reshape(1, 1),
     )
-    c1, c2 = factor[0], factor[1]
     return initial_guess + c1 * r0 - c2 * w, r0 - c1 * w + c2 * u
 
 

time: 30.2 us -> 30.2 us (level)
  no operation moved by 1% of the time
where the time goes in v8:
time: 30.2 us; the launch traced here: 30.1 us
  Pallas kernels  28 us (93%)
  between operations  1.3 us (4%)
  other arithmetic  0.74 us (2%)
    pallas_call x1, Pallas kernels, body(): pl.pallas_call(kernel, out_shape=(slab, slab, slab) + (pltpu.VMEM((1, COL...  28 us
    add x1, other arithmetic, body(): return (initial_guess + c1 * r0 - c2 * w, r0 - c1 * w + c2 * u)  0.74 us

profile of v8, /device:TPU:1, one launch (start us, length us, event | category | flops | bytes accessed | tf_op | source)
XLA Modules:
  0.0 30.1 jit_solution(8758548850148287101)
XLA Ops:
  1.3 0.0 copy-start
  1.3 28.0 %shard_map.86 = (f32[4,64,128]{2,1,0:T(8,128)S(1)}, f32[4,64,128]{2,1,0:T(8,128)S(1)}, f32[4,64,128]{2,1,0:T(8,128)S(1)}, f32[1,128]{1,0:T(1,128)S(1)}, f32[1,128]{1,0:T(1,128)S(1)}) custom-call(f32[4,64,128]{2,1,0:T(8,128)} %right_in.1, f32[4,64,128]{2,1,0:T(8,128)} %guess_in.1, s32[3,2048]{1,0:T(4,128)} %cell_in.1, f32[3,2048]{1,0:T(4,128)} %offset_in.1, ...), custom_call_target="tpu_custom_call" | custom-call | flops 3000000000 | bytes 700000 | tf_op jit(solution)/shard_map/pallas_call | solution.py:400
  29.3 0.0 copy-done
  29.4 0.7 %multiply_add_fusion = (f32[4,64,128]{2,1,0:T(8,128)}, f32[4,64,128]{2,1,0:T(8,128)}) fusion(f32[4,64,128]{2,1,0:T(8,128)S(1)} %get-tuple-element.11, f32[4,64,128]{2,1,0:T(8,128)S(1)} %get-tuple-element.8, f32[4,64,128]{2,1,0:T(8,128)S(1)} %get-tuple-element.10, f32[128]{0:T(128)S(1)} %bitcast.7, f32[128]{0:T(128)S(1)} %bitcast.6, f32[4,64,128]{2,1,0:T(8,128)S(1)} %copy-done), kind=kLoop, calls=%fused_computation | loop fusion | flops 262144 | bytes 787456 | tf_op jit(solution)/shard_map/add | solution.py:441
Async XLA Ops:
  1.3 28.1 %copy-start = (f32[4,64,128]{2,1,0:T(8,128)S(1)}, f32[4,64,128]{2,1,0:T(8,128)}, u32[]{:S(2)}) copy-start(f32[4,64,128]{2,1,0:T(8,128)} %guess_in.1) | copy-start | bytes 393220
